TPU v7x, 32 devices: a whole 2x2x4 slice. The times are simulated.
32 devices in a mesh: slab: 4 (over y, core), tile: 8 (over z, x).
Axes of the slice: x: 2, y: 2, z: 4, core: 2. Of those that a mesh axis runs over, the one named last changes fastest.
Arguments:
- positions: float32 [3, 65536], P(None, ('slab', 'tile')), may hold values from -6 to 6
- radius: float32 [65536], P(('slab', 'tile')), may hold values from 0.7 to 1.4
- uptake_rate: float32 [65536], P(('slab', 'tile')), may hold values from 0.3 to 3
- voxel_local: int32 [65536], P(('slab', 'tile')), may hold values from 0 to 262143
- cell_counts: int32 [32], P(('slab', 'tile')), may hold values from 512 to 2048, as said below
- send_counts: int32 [32, 8], P(('slab', 'tile')), may hold values from 0 to 512, as said below
- neighbor_blocks: int32 [512, 8], P(('slab', 'tile')), may hold values from 0 to 23, as said below
- field: float32 [2, 32, 128, 2048], P(None, 'slab', 'tile'), may hold values from 0.2 to 2
Outputs:
- velocity: float32 [3, 65536], P(None, ('slab', 'tile'))
- field_next: float32 [2, 32, 128, 2048], P(None, 'slab', 'tile')
Inputs may be any that keep to these rules, and one draw needn't show every extreme that they name: `cell_counts`: A multiple of 128; in every slab one tile holds 2048 live cells and another 2048 // 4. `send_counts`: row g sums to cell_counts[g]; in every slab all tiles send exactly 512 cells to one common destination tile. `neighbor_blocks`: row g * 16 + b names 8 different blocks of tile g's extended table, the first being 4 + b.
All inputs are finite; a program needn't handle non-finite values.
Results may differ from a plain program's by a relative error of at most 0.0003.
Values sent between devices are 32-bit elements; how exact they have to be, the bound alone decides.
A program may use at most 64 MiB of HBM per device.

v0:
```python
import jax
import jax.numpy as jnp
from jax import lax
from jax.sharding import PartitionSpec as P

HB = 4
K = 8
ITERS = 4


MICHAELIS_HALF = 0.5
HYPOXIA_HALF = 0.6
SECRETION = 0.4
STEP_TIME = 0.5
DIFFUSION = (0.16, 0.12)
DECAY = (0.0, 0.03)
REPULSION = 1.0
ADHESION = 0.35
REPEL_RANGE = 1.0
ADHERE_RANGE = 4.0
FORCE_SCALE = 0.08
CHEMOTAXIS = 1.5
SLOT_BLOCK = 512


def with_halo(block, sides, width):
    for axis, dim in sides:
        count = lax.axis_size(axis)
        forward = [(i, i + 1) for i in range(count - 1)]
        backward = [(target, source) for source, target in forward]
        low = lax.ppermute(
            lax.slice_in_dim(block, block.shape[dim] - width, None, axis=dim), axis, forward
        )
        high = lax.ppermute(lax.slice_in_dim(block, 0, width, axis=dim), axis, backward)
        block = jnp.concatenate([low, block, high], axis=dim)
    return block


def block_force(mine, others):
    offset = mine[:3, :, :, None, None] - others[:3, :, None, :, :]
    distance = jnp.sum(offset * offset, axis=0)
    strength = REPULSION * jnp.exp(-distance / REPEL_RANGE) - ADHESION * jnp.exp(
        -distance / ADHERE_RANGE
    )
    weight = mine[3][:, :, None, None] * others[3][:, None, :, :] * strength
    return jnp.sum(offset * weight[None], axis=(3, 4))


def relax(padded):
    center = padded[:, 1:-1, 1:-1]
    sideways = jnp.pad(center, ((0, 0), (0, 0), (0, 0), (1, 1)))
    beside_all = padded[:, 2:, 1:-1] + padded[:, :-2, 1:-1]
    beside_all = beside_all + padded[:, 1:-1, 2:] + padded[:, 1:-1, :-2]
    beside_all = beside_all + sideways[..., 2:] + sideways[..., :-2]
    spread = jnp.array(DIFFUSION, jnp.float32)[:, None, None, None]
    losses = jnp.array(DECAY, jnp.float32)[:, None, None, None]
    return center + spread * (beside_all - 6.0 * center) - losses * center


def routing(sends, length):
    ends = jnp.cumsum(sends)
    starts = ends - sends
    cell = jnp.arange(length, dtype=jnp.int32)
    target = jnp.sum((ends[:, None] <= cell[None, :]).astype(jnp.int32), axis=0)
    routed = target < sends.shape[0]
    target = jnp.minimum(target, sends.shape[0] - 1)
    lanes = jnp.arange(sends.shape[0], dtype=jnp.int32)
    first = jnp.sum(jnp.where(lanes[:, None] == target[None, :], starts[:, None], 0), axis=0)
    return (target, cell - first, routed)


def hot_tables(piece, planes, columns):
    row_hot = (piece[:, None] // columns == jnp.arange(planes, dtype=jnp.int32)[None, :]).astype(
        jnp.float32
    )
    column_hot = (piece[:, None] % columns == jnp.arange(columns, dtype=jnp.int32)[None, :]).astype(
        jnp.float32
    )
    return (row_hot, column_hot)


def pick_voxels(fields, reached):
    species, planes, columns = fields.shape
    pieces = reached.reshape(-1, SLOT_BLOCK)

    def one_piece(piece):
        row_hot, column_hot = hot_tables(piece, planes, columns)
        picked = jnp.einsum("srx,mx->srm", fields, column_hot, precision=lax.Precision.HIGHEST)
        return jnp.sum(picked * jnp.transpose(row_hot)[None], axis=1)

    found = lax.map(one_piece, pieces)
    return jnp.moveaxis(found, 1, 0).reshape(species, -1)


def spread_voxels(amounts, reached, planes, columns):
    species = amounts.shape[0]
    pieces = reached.reshape(-1, SLOT_BLOCK)
    shares = jnp.moveaxis(amounts.reshape(species, -1, SLOT_BLOCK), 1, 0)

    def add_piece(total, item):
        piece, share = item
        row_hot, column_hot = hot_tables(piece, planes, columns)
        weighted = share[:, :, None] * row_hot[None]
        return (
            total
            + jnp.einsum("smr,mx->srx", weighted, column_hot, precision=lax.Precision.HIGHEST),
            None,
        )

    empty = jnp.zeros((species, planes, columns), jnp.float32)
    total, unused = lax.scan(add_piece, empty, (pieces, shares))
    return total


def local(
    positions, radius, uptake_rate, voxel_local, cell_counts, send_counts, neighbor_blocks, field
):
    tiles = lax.axis_size("tile")
    capacity = positions.shape[1]
    blocks = capacity // 128
    slot_size = 2 * capacity // tiles
    cell = jnp.arange(capacity, dtype=jnp.int32)
    count = cell_counts[0]
    kept = jnp.where(cell < count, radius, 0.0)
    table = jnp.concatenate([positions, kept[None]], axis=0)
    extended = with_halo(table, (("tile", 1),), HB * 128)
    extended = extended.reshape(4, blocks + 2 * HB, 128)
    group = 4
    turns = (count // 128 + group - 1) // group

    def one_turn(turn, total):
        first = turn * group
        chosen = lax.dynamic_slice_in_dim(neighbor_blocks, first, group, 0)
        mine = lax.dynamic_slice_in_dim(extended, first + HB, group, 1)
        others = jnp.take(extended, chosen.reshape(-1), axis=1).reshape(4, group, K, 128)
        return lax.dynamic_update_slice_in_dim(total, block_force(mine, others), first, 1)

    forces = lax.fori_loop(0, turns, one_turn, jnp.zeros((3, blocks, 128), jnp.float32))
    forces = forces.reshape(3, capacity)
    sends = send_counts[0]
    ends = jnp.cumsum(sends)
    starts = ends - sends
    ranks = jnp.arange(slot_size, dtype=jnp.int32)
    valid = ranks[None, :] < sends[:, None]
    source = jnp.where(valid, starts[:, None] + ranks[None, :], 0)
    wanted = jnp.where(valid, jnp.take(voxel_local, source), 0)
    rates = jnp.where(valid, jnp.take(uptake_rate, source), 0.0)
    species, depth, rows, columns = field.shape
    planes = depth * rows
    oxygen_rows = field[0].reshape(1, planes, columns)
    packed = jnp.stack([wanted.astype(jnp.float32), rates])
    unpacked = lax.all_to_all(packed, "tile", split_axis=1, concat_axis=1, tiled=True)
    reached = unpacked[0].astype(jnp.int32).reshape(-1)
    given = unpacked[1]
    oxygen = pick_voxels(oxygen_rows, reached).reshape(tiles, slot_size)
    consume = given * oxygen / (MICHAELIS_HALF + oxygen)
    secrete = SECRETION * given * HYPOXIA_HALF / (HYPOXIA_HALF + oxygen)
    arrived = jnp.stack([-STEP_TIME * consume, STEP_TIME * secrete])
    added = spread_voxels(arrived.reshape(species, -1), reached, planes, columns)
    state = field + added.reshape(species, depth, rows, columns)
    for step in range(ITERS):
        state = relax(with_halo(state, (("slab", 1), ("tile", 2)), 1))
    border = with_halo(state[1], (("slab", 0), ("tile", 1)), 1)
    rise_z = 0.5 * (border[2:, 1:-1] - border[:-2, 1:-1])
    rise_y = 0.5 * (border[1:-1, 2:] - border[1:-1, :-2])
    middle = jnp.pad(border[1:-1, 1:-1], ((0, 0), (0, 0), (1, 1)))
    rise_x = 0.5 * (middle[..., 2:] - middle[..., :-2])
    rises = jnp.stack([rise_z, rise_y, rise_x]).reshape(3, planes, columns)
    slopes = pick_voxels(rises, reached).reshape(3, tiles, slot_size)
    returned = lax.all_to_all(slopes, "tile", split_axis=1, concat_axis=1, tiled=True)
    target, rank, routed = routing(sends, capacity)
    where_back = jnp.clip(target * slot_size + rank, 0, tiles * slot_size - 1)
    slope = jnp.take(returned.reshape(3, tiles * slot_size), where_back, axis=1)
    slope = jnp.where(routed[None, :], slope, 0.0)
    velocity = FORCE_SCALE * forces + CHEMOTAXIS * slope
    return (velocity, state)


def solution(mesh):
    placed = (
        P(None, ("slab", "tile")),
        P(("slab", "tile")),
        P(("slab", "tile")),
        P(("slab", "tile")),
        P(("slab", "tile")),
        P(("slab", "tile"), None),
        P(("slab", "tile"), None),
        P(None, "slab", "tile", None),
    )
    return jax.shard_map(
        local,
        mesh=mesh,
        in_specs=placed,
        out_specs=(P(None, ("slab", "tile")), P(None, "slab", "tile", None)),
        check_vma=False,
    )
```

profile of v0, /device:TPU:0, one launch (start us, length us, event | category | flops | bytes accessed | tf_op | source)
XLA Modules:
  0.0 365.3 jit_solution(255518359361342819)
XLA Ops:
  2.9 23.0 %gather_fusion.1 = s32[4096]{0:T(1024)S(1)} fusion(s32[2048]{0:T(1024)S(1)} %copy-done, s32[4096]{0:T(1024)S(1)} %broadcast_clamp_fusion), kind=kCustom, calls=%fused_computation.1 | custom fusion | bytes 49152 | tf_op jit(solution)/shard_map/jit(_take)/gather | solution.py:146
  26.7 23.0 %gather_fusion.2 = f32[4096]{0:T(1024)S(1)} fusion(f32[2048]{0:T(1024)S(1)} %copy-done.1, s32[4096]{0:T(1024)S(1)} %broadcast_clamp_fusion), kind=kCustom, calls=%fused_computation.2 | custom fusion | bytes 49152 | tf_op jit(solution)/shard_map/jit(_take)/gather | solution.py:147
  50.5 7.3 %all-to-all-start = ((f32[2,8,512]{2,0,1:T(2,128)}), f32[2,8,512]{2,0,1:T(2,128)S(1)}, u32[]{:S(2)}, u32[]{:S(2)}) async-start(f32[2,8,512]{2,0,1:T(2,128)} %pad_maximum_fusion.56), calls=%async_computation | async-start | bytes 65536 | tf_op jit(solution)/shard_map/all_to_all | solution.py:152
  57.7 6.7 %all-to-all-done = f32[2,8,512]{2,0,1:T(2,128)S(1)} async-done(((f32[2,8,512]{2,0,1:T(2,128)}), f32[2,8,512]{2,0,1:T(2,128)S(1)}, u32[]{:S(2)}, u32[]{:S(2)}) %all-to-all-start) | async-done | bytes 32800 | tf_op jit(solution)/shard_map/all_to_all | solution.py:152
  64.5 20.6 %while.50 = (s32[]{:T(128)}, f32[8,1,512]{2,1,0:T(1,128)S(1)}, s32[8,512]{1,0:T(8,128)S(1)}, f32[1,128,2048]{2,1,0:T(8,128)S(1)}, s32[]{:T(128)}) while((s32[]{:T(128)}, f32[8,1,512]{2,1,0:T(1,128)S(1)}, s32[8,512]{1,0:T(8,128)S(1)}, f32[1,128,2048]{2,1,0:T(8,128)S(1)}, s32[]{:T(128)}) %tuple.147), condition=%wide.region_9.10_spmd, body=%wide.region_7.9_spmd.sunk | while | flops 1611867136 | bytes 1069125 | solution.py:91
  85.2 25.0 %while.52 = (s32[]{:T(128)}, f32[2,128,2048]{2,1,0:T(8,128)S(1)}, f32[8,2,512]{2,1,0:T(2,128)S(1)}, s32[8,512]{1,0:T(8,128)S(1)}, s32[]{:T(128)}, /*index=5*/s32[]{:T(128)}) while((s32[]{:T(128)}, f32[2,128,2048]{2,1,0:T(8,128)S(1)}, f32[8,2,512]{2,1,0:T(2,128)S(1)}, s32[8,512]{1,0:T(8,128)S(1)}, s32[]{:T(128)}, ...), condition=%wide.region_11.12_spmd.clone, body=%wide.region_10.11_spmd.clone.sunk | while | flops 3223594496 | bytes 4745303 | solution.py:111
  85.3 3.0 fusion.115
  88.4 3.0 fusion.115
  91.5 3.0 fusion.115
  94.7 3.0 fusion.115
  97.8 3.0 fusion.115
  100.9 3.0 fusion.115
  104.0 3.0 fusion.115
  107.1 3.0 fusion.115
  113.6 3.0 collective-permute-start.3
  119.4 4.6 %collective-permute-start.5 = (f32[2,10,1,2048]{3,1,2,0:T(8,128)S(1)}, f32[2,10,1,2048]{3,1,2,0:T(8,128)S(1)}, u32[]{:S(2)}, u32[]{:S(2)}) collective-permute-start(f32[2,10,1,2048]{3,1,2,0:T(8,128)S(1)} %copy.66), channel_id=1, source_target_pairs={{0,1},{1,2},{2,3},{3,4},{4,5},{5,6},{6,7},{8,9},{9,10},{10,11},{11... | collective-permute-start | bytes 491528 | tf_op jit(solution)/shard_map/ppermute | solution.py:31
  124.0 2.8 collective-permute-done.4
  126.9 6.6 %collective-permute-done.5 = f32[2,10,1,2048]{3,1,2,0:T(8,128)S(1)} collective-permute-done((f32[2,10,1,2048]{3,1,2,0:T(8,128)S(1)}, f32[2,10,1,2048]{3,1,2,0:T(8,128)S(1)}, u32[]{:S(2)}, u32[]{:S(2)}) %collective-permute-start.5) | collective-permute-done | bytes 163872 | tf_op jit(solution)/shard_map/ppermute | solution.py:31
  133.7 2.7 fusion.42
  137.7 3.0 collective-permute-start.7
  143.6 5.0 %collective-permute-start.9 = (f32[2,10,1,2048]{3,1,2,0:T(8,128)S(1)}, f32[2,10,1,2048]{3,1,2,0:T(8,128)S(1)}, u32[]{:S(2)}, u32[]{:S(2)}) collective-permute-start(f32[2,10,1,2048]{3,1,2,0:T(8,128)S(1)} %copy.70), channel_id=1, source_target_pairs={{0,1},{1,2},{2,3},{3,4},{4,5},{5,6},{6,7},{8,9},{9,10},{10,11},{11... | collective-permute-start | bytes 491528 | tf_op jit(solution)/shard_map/ppermute | solution.py:31
  151.1 8.6 %collective-permute-done.9 = f32[2,10,1,2048]{3,1,2,0:T(8,128)S(1)} collective-permute-done((f32[2,10,1,2048]{3,1,2,0:T(8,128)S(1)}, f32[2,10,1,2048]{3,1,2,0:T(8,128)S(1)}, u32[]{:S(2)}, u32[]{:S(2)}) %collective-permute-start.9) | collective-permute-done | bytes 163872 | tf_op jit(solution)/shard_map/ppermute | solution.py:31
  159.9 2.7 fusion.48
  163.9 3.0 collective-permute-start.11
  167.0 4.4 %collective-permute-start = (f32[4,512]{1,0:T(4,128)S(1)}, f32[4,512]{1,0:T(4,128)S(1)}, u32[]{:S(2)}, u32[]{:S(2)}) collective-permute-start(f32[4,512]{1,0:T(4,128)S(1)} %get-tuple-element.365), channel_id=1, source_target_pairs={{0,1},{1,2},{2,3},{3,4},{4,5},{5,6},{6,7},{8,9},{9,10},{10,11},{11... | collective-permute-start | bytes 24584 | tf_op jit(solution)/shard_map/ppermute | solution.py:31
  174.7 5.2 %collective-permute-start.13 = (f32[2,10,1,2048]{3,1,2,0:T(8,128)S(1)}, f32[2,10,1,2048]{3,1,2,0:T(8,128)S(1)}, u32[]{:S(2)}, u32[]{:S(2)}) collective-permute-start(f32[2,10,1,2048]{3,1,2,0:T(8,128)S(1)} %copy.74), channel_id=1, source_target_pairs={{0,1},{1,2},{2,3},{3,4},{4,5},{5,6},{6,7},{8,9},{9,10},{10,11},{11... | collective-permute-start | bytes 491528 | tf_op jit(solution)/shard_map/ppermute | solution.py:31
  180.0 4.9 %collective-permute-done.12 = f32[2,10,1,2048]{3,1,2,0:T(8,128)S(1)} collective-permute-done((f32[2,10,1,2048]{3,1,2,0:T(8,128)S(1)}, f32[2,10,1,2048]{3,1,2,0:T(8,128)S(1)}, u32[]{:S(2)}, u32[]{:S(2)}) %collective-permute-start.12) | collective-permute-done | bytes 163872 | tf_op jit(solution)/shard_map/ppermute | solution.py:34
  185.1 5.8 %collective-permute-done.13 = f32[2,10,1,2048]{3,1,2,0:T(8,128)S(1)} collective-permute-done((f32[2,10,1,2048]{3,1,2,0:T(8,128)S(1)}, f32[2,10,1,2048]{3,1,2,0:T(8,128)S(1)}, u32[]{:S(2)}, u32[]{:S(2)}) %collective-permute-start.13) | collective-permute-done | bytes 163872 | tf_op jit(solution)/shard_map/ppermute | solution.py:31
  195.1 3.0 collective-permute-start.15
  201.7 5.7 %collective-permute-start.17 = (f32[2,10,1,2048]{3,1,2,0:T(8,128)}, f32[2,10,1,2048]{3,1,2,0:T(8,128)}, u32[]{:S(2)}, u32[]{:S(2)}) collective-permute-start(f32[2,10,1,2048]{3,1,2,0:T(8,128)} %copy.78), channel_id=1, source_target_pairs={{0,1},{1,2},{2,3},{3,4},{4,5},{5,6},{6,7},{8,9},{9,10},{10,11},{11... | collective-permute-start | bytes 491528 | tf_op jit(solution)/shard_map/ppermute | solution.py:31
  208.5 8.7 %collective-permute-done.17 = f32[2,10,1,2048]{3,1,2,0:T(8,128)} collective-permute-done((f32[2,10,1,2048]{3,1,2,0:T(8,128)}, f32[2,10,1,2048]{3,1,2,0:T(8,128)}, u32[]{:S(2)}, u32[]{:S(2)}) %collective-permute-start.17) | collective-permute-done | bytes 163872 | tf_op jit(solution)/shard_map/ppermute | solution.py:31
  222.3 3.0 collective-permute-start.19
  228.4 5.7 %collective-permute-start.21 = (f32[10,1,2048]{2,1,0:T(1,128)}, f32[10,1,2048]{2,1,0:T(1,128)}, u32[]{:S(2)}, u32[]{:S(2)}) collective-permute-start(f32[10,1,2048]{2,1,0:T(1,128)} %get-tuple-element.361), channel_id=1, source_target_pairs={{0,1},{1,2},{2,3},{3,4},{4,5},{5,6},{6,7},{8,9},{9,10},{10,11},{11... | collective-permute-start | bytes 245768 | tf_op jit(solution)/shard_map/ppermute | solution.py:31
  234.1 18.9 %while.49 = (s32[]{:T(128)}, f32[3,16,128]{2,1,0:T(8,128)S(1)}, s32[]{:T(128)}, f32[4,24,128]{2,0,1:T(4,128)S(1)}, s32[16,8]{1,0:T(8,128)S(1)}, /*index=5*/s32[]...) while((s32[]{:T(128)}, f32[3,16,128]{2,1,0:T(8,128)S(1)}, s32[]{:T(128)}, ...), condition=%wide.region_3.4_spmd, body=%wide.region_0.3_spmd.sunk | while | flops 12074795 | bytes 8963753 | solution.py:138
  237.9 15.0 %fusion.105 = f32[3,4,128]{2,1,0:T(4,128)S(1)} fusion(f32[4,128,8,128]{3,2,1,0:T(8,128)S(1)} %subtract_multiply_fusion.4, f32[3,4,8,128]{3,2,1,0:T(8,128)S(1)} %copy.88, f32[3,4,128]{2,1,0:T(4,128)S(1)} %copy.89), kind=kLoop, calls=%fused_computation.44.clone.1 | loop fusion | flops 4717056 | bytes 2158592 | tf_op jit(solution)/shard_map/while/body/reduce_sum | solution.py:46
  255.1 30.7 %while.51 = (s32[]{:T(128)}, f32[8,3,512]{2,1,0:T(4,128)}, s32[8,512]{1,0:T(8,128)S(1)}, f32[3,128,2048]{2,1,0:T(8,128)S(1)}, s32[]{:T(128)}) while((s32[]{:T(128)}, f32[8,3,512]{2,1,0:T(4,128)}, s32[8,512]{1,0:T(8,128)S(1)}, f32[3,128,2048]{2,1,0:T(8,128)S(1)}, s32[]{:T(128)}) %tuple.149), condition=%wide.region_14.15_spmd, body=%wide.region_12.14_spmd.sunk | while | flops 4833419264 | bytes 3705409 | solution.py:91
  255.2 3.2 fusion.111
  259.0 3.2 fusion.111
  262.8 3.2 fusion.111
  266.7 3.2 fusion.111
  270.5 3.2 fusion.111
  274.3 3.2 fusion.111
  278.2 3.2 fusion.111
  282.0 3.2 fusion.111
  285.8 60.4 %all-to-all-start.1 = ((f32[3,8,512]{2,0,1:T(4,128)}), f32[3,8,512]{2,0,1:T(4,128)S(1)}, u32[]{:S(2)}, u32[]{:S(2)}) async-start(f32[3,8,512]{2,0,1:T(4,128)} %bitcast.32), calls=%async_computation.1 | async-start | bytes 131072 | tf_op jit(solution)/shard_map/all_to_all | solution.py:170
  346.6 6.6 %all-to-all-done.1 = f32[3,8,512]{2,0,1:T(4,128)S(1)} async-done(((f32[3,8,512]{2,0,1:T(4,128)}), f32[3,8,512]{2,0,1:T(4,128)S(1)}, u32[]{:S(2)}, u32[]{:S(2)}) %all-to-all-start.1) | async-done | bytes 49184 | tf_op jit(solution)/shard_map/all_to_all | solution.py:170
  353.9 7.6 %gather_fusion.3 = f32[2048,3]{1,0:T(8,128)} fusion(f32[3,4096]{0,1:T(8,128)S(1)} %bitcast.147, s32[2048]{0:T(1024)S(1)} %broadcast_clamp_fusion.1), kind=kCustom, calls=%fused_computation.3 | custom fusion | bytes 57344 | tf_op jit(solution)/shard_map/jit(_take)/gather | solution.py:173
  361.5 2.9 bitcast_add_fusion
  (223 shorter events, 71.8 us)
Async XLA Ops:
  0.6 2.3 copy-start
  2.9 23.1 %copy-start.8 = (s32[1,8]{1,0:T(1,128)S(1)}, s32[1,8]{1,0:T(1,128)}, u32[]{:S(2)}) copy-start(s32[1,8]{1,0:T(1,128)} %param.29) | copy-start | bytes 100
  26.0 0.7 copy-start.1
  49.7 14.8 %slice-start = ((f32[2,8,16,2048]{3,2,1,0:T(8,128)}), f32[1,8,16,2048]{3,2,1,0:T(8,128)S(1)}, s32[]{:S(2)}) async-start(f32[2,8,16,2048]{3,2,1,0:T(8,128)} %param.31), calls=%async_computation.2 | async-start | bytes 2097152 | tf_op jit(solution)/shard_map/slice | solution.py:150
  50.5 13.9 %all-to-all-start = ((f32[2,8,512]{2,0,1:T(2,128)}), f32[2,8,512]{2,0,1:T(2,128)S(1)}, u32[]{:S(2)}, u32[]{:S(2)}) async-start(f32[2,8,512]{2,0,1:T(2,128)} %pad_maximum_fusion.56), calls=%async_computation | async-start | bytes 65536 | tf_op jit(solution)/shard_map/all_to_all | solution.py:152
  112.2 4.4 %collective-permute-start.2 = (f32[2,1,16,2048]{3,2,1,0:T(8,128)S(1)}, f32[2,1,16,2048]{3,2,1,0:T(8,128)S(1)}, u32[]{:S(2)}, u32[]{:S(2)}) collective-permute-start(f32[2,1,16,2048]{3,2,1,0:T(8,128)S(1)} %get-tuple-element.357), channel_id=1, source_target_pairs={{8,0},{16,8},{24,16},{9,1},{17,9},{25,17},{10,2},{18,10},{26,18},{... | collective-permute-start | bytes 786440 | tf_op jit(solution)/shard_map/ppermute | solution.py:34
  113.5 20.2 %copy-start.5 = (f32[2]{0:T(128)S(1)}, f32[2]{0:T(128)}, u32[]{:S(2)}) copy-start(f32[2]{0:T(128)} %constant.345.clone) | copy-start | bytes 28
  113.5 20.2 %copy-start.6 = (f32[2]{0:T(128)S(1)}, f32[2]{0:T(128)}, u32[]{:S(2)}) copy-start(f32[2]{0:T(128)} %constant.346.clone) | copy-start | bytes 28
  113.6 4.2 %collective-permute-start.3 = (f32[2,1,16,2048]{3,2,1,0:T(8,128)S(1)}, f32[2,1,16,2048]{3,2,1,0:T(8,128)S(1)}, u32[]{:S(2)}, u32[]{:S(2)}) collective-permute-start(f32[2,1,16,2048]{3,2,1,0:T(8,128)S(1)} %get-tuple-element.356), channel_id=1, source_target_pairs={{0,8},{8,16},{16,24},{1,9},{9,17},{17,25},{2,10},{10,18},{18,26},{... | collective-permute-start | bytes 786440 | tf_op jit(solution)/shard_map/ppermute | solution.py:31
  118.1 8.7 %collective-permute-start.4 = (f32[2,10,1,2048]{3,1,2,0:T(8,128)S(1)}, f32[2,10,1,2048]{3,1,2,0:T(8,128)S(1)}, u32[]{:S(2)}, u32[]{:S(2)}) collective-permute-start(f32[2,10,1,2048]{3,1,2,0:T(8,128)S(1)} %copy.64), channel_id=1, source_target_pairs={{1,0},{2,1},{3,2},{4,3},{5,4},{6,5},{7,6},{9,8},{10,9},{11,10},{12... | collective-permute-start | bytes 491528 | tf_op jit(solution)/shard_map/ppermute | solution.py:34
  119.4 14.1 %collective-permute-start.5 = (f32[2,10,1,2048]{3,1,2,0:T(8,128)S(1)}, f32[2,10,1,2048]{3,1,2,0:T(8,128)S(1)}, u32[]{:S(2)}, u32[]{:S(2)}) collective-permute-start(f32[2,10,1,2048]{3,1,2,0:T(8,128)S(1)} %copy.66), channel_id=1, source_target_pairs={{0,1},{1,2},{2,3},{3,4},{4,5},{5,6},{6,7},{8,9},{9,10},{10,11},{11... | collective-permute-start | bytes 491528 | tf_op jit(solution)/shard_map/ppermute | solution.py:31
  136.4 4.4 %collective-permute-start.6 = (f32[2,1,16,2048]{3,2,1,0:T(8,128)S(1)}, f32[2,1,16,2048]{3,2,1,0:T(8,128)S(1)}, u32[]{:S(2)}, u32[]{:S(2)}) collective-permute-start(f32[2,1,16,2048]{3,2,1,0:T(8,128)S(1)} %get-tuple-element.355), channel_id=1, source_target_pairs={{8,0},{16,8},{24,16},{9,1},{17,9},{25,17},{10,2},{18,10},{26,18},{... | collective-permute-start | bytes 786440 | tf_op jit(solution)/shard_map/ppermute | solution.py:34
  137.7 4.2 %collective-permute-start.7 = (f32[2,1,16,2048]{3,2,1,0:T(8,128)S(1)}, f32[2,1,16,2048]{3,2,1,0:T(8,128)S(1)}, u32[]{:S(2)}, u32[]{:S(2)}) collective-permute-start(f32[2,1,16,2048]{3,2,1,0:T(8,128)S(1)} %get-tuple-element.354), channel_id=1, source_target_pairs={{0,8},{8,16},{16,24},{1,9},{9,17},{17,25},{2,10},{10,18},{18,26},{... | collective-permute-start | bytes 786440 | tf_op jit(solution)/shard_map/ppermute | solution.py:31
  142.2 8.7 %collective-permute-start.8 = (f32[2,10,1,2048]{3,1,2,0:T(8,128)S(1)}, f32[2,10,1,2048]{3,1,2,0:T(8,128)S(1)}, u32[]{:S(2)}, u32[]{:S(2)}) collective-permute-start(f32[2,10,1,2048]{3,1,2,0:T(8,128)S(1)} %copy.68), channel_id=1, source_target_pairs={{1,0},{2,1},{3,2},{4,3},{5,4},{6,5},{7,6},{9,8},{10,9},{11,10},{12... | collective-permute-start | bytes 491528 | tf_op jit(solution)/shard_map/ppermute | solution.py:34
  143.6 16.1 %collective-permute-start.9 = (f32[2,10,1,2048]{3,1,2,0:T(8,128)S(1)}, f32[2,10,1,2048]{3,1,2,0:T(8,128)S(1)}, u32[]{:S(2)}, u32[]{:S(2)}) collective-permute-start(f32[2,10,1,2048]{3,1,2,0:T(8,128)S(1)} %copy.70), channel_id=1, source_target_pairs={{0,1},{1,2},{2,3},{3,4},{4,5},{5,6},{6,7},{8,9},{9,10},{10,11},{11... | collective-permute-start | bytes 491528 | tf_op jit(solution)/shard_map/ppermute | solution.py:31
  159.9 7.1 %copy-start.7 = (f32[2048]{0:T(1024)S(1)}, f32[2048]{0:T(1024)}, u32[]{:S(2)}) copy-start(f32[2048]{0:T(1024)} %param.25) | copy-start | bytes 24580
  159.9 7.1 %copy-start.4 = (f32[3,2048]{1,0:T(4,128)S(1)}, f32[3,2048]{1,0:T(4,128)}, u32[]{:S(2)}) copy-start(f32[3,2048]{1,0:T(4,128)} %param.24) | copy-start | bytes 73732
  162.6 10.2 %collective-permute-start.10 = (f32[2,1,16,2048]{3,2,1,0:T(8,128)S(1)}, f32[2,1,16,2048]{3,2,1,0:T(8,128)S(1)}, u32[]{:S(2)}, u32[]{:S(2)}) collective-permute-start(f32[2,1,16,2048]{3,2,1,0:T(8,128)S(1)} %get-tuple-element.353), channel_id=1, source_target_pairs={{8,0},{16,8},{24,16},{9,1},{17,9},{25,17},{10,2},{18,10},{26,18},{... | collective-permute-start | bytes 786440 | tf_op jit(solution)/shard_map/ppermute | solution.py:34
  163.9 8.9 %collective-permute-start.11 = (f32[2,1,16,2048]{3,2,1,0:T(8,128)S(1)}, f32[2,1,16,2048]{3,2,1,0:T(8,128)S(1)}, u32[]{:S(2)}, u32[]{:S(2)}) collective-permute-start(f32[2,1,16,2048]{3,2,1,0:T(8,128)S(1)} %get-tuple-element.352), channel_id=1, source_target_pairs={{0,8},{8,16},{16,24},{1,9},{9,17},{17,25},{2,10},{10,18},{18,26},{... | collective-permute-start | bytes 786440 | tf_op jit(solution)/shard_map/ppermute | solution.py:31
  167.0 40.4 %collective-permute-start = (f32[4,512]{1,0:T(4,128)S(1)}, f32[4,512]{1,0:T(4,128)S(1)}, u32[]{:S(2)}, u32[]{:S(2)}) collective-permute-start(f32[4,512]{1,0:T(4,128)S(1)} %get-tuple-element.365), channel_id=1, source_target_pairs={{0,1},{1,2},{2,3},{3,4},{4,5},{5,6},{6,7},{8,9},{9,10},{10,11},{11... | collective-permute-start | bytes 24584 | tf_op jit(solution)/shard_map/ppermute | solution.py:31
  171.4 36.0 %collective-permute-start.1 = (f32[4,512]{1,0:T(4,128)S(1)}, f32[4,512]{1,0:T(4,128)S(1)}, u32[]{:S(2)}, u32[]{:S(2)}) collective-permute-start(f32[4,512]{1,0:T(4,128)S(1)} %get-tuple-element.366), channel_id=1, source_target_pairs={{1,0},{2,1},{3,2},{4,3},{5,4},{6,5},{7,6},{9,8},{10,9},{11,10},{12... | collective-permute-start | bytes 24584 | tf_op jit(solution)/shard_map/ppermute | solution.py:34
  173.2 11.8 %collective-permute-start.12 = (f32[2,10,1,2048]{3,1,2,0:T(8,128)S(1)}, f32[2,10,1,2048]{3,1,2,0:T(8,128)S(1)}, u32[]{:S(2)}, u32[]{:S(2)}) collective-permute-start(f32[2,10,1,2048]{3,1,2,0:T(8,128)S(1)} %copy.72), channel_id=1, source_target_pairs={{1,0},{2,1},{3,2},{4,3},{5,4},{6,5},{7,6},{9,8},{10,9},{11,10},{12... | collective-permute-start | bytes 491528 | tf_op jit(solution)/shard_map/ppermute | solution.py:34
  174.7 16.2 %collective-permute-start.13 = (f32[2,10,1,2048]{3,1,2,0:T(8,128)S(1)}, f32[2,10,1,2048]{3,1,2,0:T(8,128)S(1)}, u32[]{:S(2)}, u32[]{:S(2)}) collective-permute-start(f32[2,10,1,2048]{3,1,2,0:T(8,128)S(1)} %copy.74), channel_id=1, source_target_pairs={{0,1},{1,2},{2,3},{3,4},{4,5},{5,6},{6,7},{8,9},{9,10},{10,11},{11... | collective-permute-start | bytes 491528 | tf_op jit(solution)/shard_map/ppermute | solution.py:31
  193.8 13.6 %copy-start.9 = (s32[16,8]{0,1:T(8,128)S(1)}, s32[16,8]{0,1:T(8,128)}, u32[]{:S(2)}) copy-start(s32[16,8]{0,1:T(8,128)} %param.30) | copy-start | bytes 1540
  193.8 4.4 %collective-permute-start.14 = (f32[2,1,16,2048]{3,2,1,0:T(8,128)S(1)}, f32[2,1,16,2048]{3,2,1,0:T(8,128)S(1)}, u32[]{:S(2)}, u32[]{:S(2)}) collective-permute-start(f32[2,1,16,2048]{3,2,1,0:T(8,128)S(1)} %get-tuple-element.351), channel_id=1, source_target_pairs={{8,0},{16,8},{24,16},{9,1},{17,9},{25,17},{10,2},{18,10},{26,18},{... | collective-permute-start | bytes 786440 | tf_op jit(solution)/shard_map/ppermute | solution.py:34
  195.1 4.2 %collective-permute-start.15 = (f32[2,1,16,2048]{3,2,1,0:T(8,128)S(1)}, f32[2,1,16,2048]{3,2,1,0:T(8,128)S(1)}, u32[]{:S(2)}, u32[]{:S(2)}) collective-permute-start(f32[2,1,16,2048]{3,2,1,0:T(8,128)S(1)} %get-tuple-element.350), channel_id=1, source_target_pairs={{0,8},{8,16},{16,24},{1,9},{9,17},{17,25},{2,10},{10,18},{18,26},{... | collective-permute-start | bytes 786440 | tf_op jit(solution)/shard_map/ppermute | solution.py:31
  199.6 8.7 %collective-permute-start.16 = (f32[2,10,1,2048]{3,1,2,0:T(8,128)S(1)}, f32[2,10,1,2048]{3,1,2,0:T(8,128)S(1)}, u32[]{:S(2)}, u32[]{:S(2)}) collective-permute-start(f32[2,10,1,2048]{3,1,2,0:T(8,128)S(1)} %copy.76), channel_id=1, source_target_pairs={{1,0},{2,1},{3,2},{4,3},{5,4},{6,5},{7,6},{9,8},{10,9},{11,10},{12... | collective-permute-start | bytes 491528 | tf_op jit(solution)/shard_map/ppermute | solution.py:34
  201.7 15.5 %collective-permute-start.17 = (f32[2,10,1,2048]{3,1,2,0:T(8,128)}, f32[2,10,1,2048]{3,1,2,0:T(8,128)}, u32[]{:S(2)}, u32[]{:S(2)}) collective-permute-start(f32[2,10,1,2048]{3,1,2,0:T(8,128)} %copy.78), channel_id=1, source_target_pairs={{0,1},{1,2},{2,3},{3,4},{4,5},{5,6},{6,7},{8,9},{9,10},{10,11},{11... | collective-permute-start | bytes 491528 | tf_op jit(solution)/shard_map/ppermute | solution.py:31
  221.0 4.4 %copy-start.2 = (f32[2,8,16,2048]{3,2,1,0:T(8,128)}, f32[2,8,16,2048]{3,2,1,0:T(8,128)S(1)}, u32[]{:S(2)}) copy-start(f32[2,8,16,2048]{3,2,1,0:T(8,128)S(1)} %fusion.60) | copy-start | bytes 6291460
  221.0 4.5 %collective-permute-start.18 = (f32[1,16,2048]{2,1,0:T(8,128)S(1)}, f32[1,16,2048]{2,1,0:T(8,128)S(1)}, u32[]{:S(2)}, u32[]{:S(2)}) collective-permute-start(f32[1,16,2048]{2,1,0:T(8,128)S(1)} %get-tuple-element.349), channel_id=1, source_target_pairs={{8,0},{16,8},{24,16},{9,1},{17,9},{25,17},{10,2},{18,10},{26,18},{... | collective-permute-start | bytes 393224 | tf_op jit(solution)/shard_map/ppermute | solution.py:34
  222.3 4.0 %collective-permute-start.19 = (f32[1,16,2048]{2,1,0:T(8,128)S(1)}, f32[1,16,2048]{2,1,0:T(8,128)S(1)}, u32[]{:S(2)}, u32[]{:S(2)}) collective-permute-start(f32[1,16,2048]{2,1,0:T(8,128)S(1)} %get-tuple-element.348), channel_id=1, source_target_pairs={{0,8},{8,16},{16,24},{1,9},{9,17},{17,25},{2,10},{10,18},{18,26},{... | collective-permute-start | bytes 393224 | tf_op jit(solution)/shard_map/ppermute | solution.py:31
  226.3 7.7 %copy-start.3 = (f32[1,16,2048]{2,1,0:T(8,128)}, f32[1,16,2048]{2,1,0:T(8,128)S(1)}, u32[]{:S(2)}) copy-start(f32[1,16,2048]{2,1,0:T(8,128)S(1)} %collective-permute-done.19) | copy-start | bytes 393220
  227.1 25.9 %collective-permute-start.20 = (f32[10,1,2048]{2,1,0:T(1,128)}, f32[10,1,2048]{2,1,0:T(1,128)}, u32[]{:S(2)}, u32[]{:S(2)}) collective-permute-start(f32[10,1,2048]{2,1,0:T(1,128)} %get-tuple-element.360), channel_id=1, source_target_pairs={{1,0},{2,1},{3,2},{4,3},{5,4},{6,5},{7,6},{9,8},{10,9},{11,10},{12... | collective-permute-start | bytes 245768 | tf_op jit(solution)/shard_map/ppermute | solution.py:34
  228.4 24.6 %collective-permute-start.21 = (f32[10,1,2048]{2,1,0:T(1,128)}, f32[10,1,2048]{2,1,0:T(1,128)}, u32[]{:S(2)}, u32[]{:S(2)}) collective-permute-start(f32[10,1,2048]{2,1,0:T(1,128)} %get-tuple-element.361), channel_id=1, source_target_pairs={{0,1},{1,2},{2,3},{3,4},{4,5},{5,6},{6,7},{8,9},{9,10},{10,11},{11... | collective-permute-start | bytes 245768 | tf_op jit(solution)/shard_map/ppermute | solution.py:31
  285.8 67.4 %all-to-all-start.1 = ((f32[3,8,512]{2,0,1:T(4,128)}), f32[3,8,512]{2,0,1:T(4,128)S(1)}, u32[]{:S(2)}, u32[]{:S(2)}) async-start(f32[3,8,512]{2,0,1:T(4,128)} %bitcast.32), calls=%async_computation.1 | async-start | bytes 131072 | tf_op jit(solution)/shard_map/all_to_all | solution.py:170
where the time goes:
time: 368 us; the launch traced here: 365 us
  starting transfers between devices  128 us (35%)
  matrix products  69.6 us (19%)
  local copies, waits for them, and re-layouts  66 us (18%)
  waiting for transfers between devices  57.4 us (16%)
  other arithmetic  41.5 us (11%)
    all_to_all x1, starting transfers between devices, local(): lax.all_to_all(slopes, 'tile', split_axis=1, concat_axis=1, tiled=True)  60.4 us
    ppermute x11, starting transfers between devices, with_halo(): lax.ppermute(lax.slice_in_dim(block, block.shape[dim] - width, None, axis...  45.7 us
    dot_general x16, matrix products, one_piece(): jnp.einsum('srx,mx->srm', fields, column_hot, precision=lax.Precision.HIG...  45.5 us
    ppermute x11, waiting for transfers between devices, with_halo(): lax.ppermute(lax.slice_in_dim(block, block.shape[dim] - width, None, axis...  33.8 us
    dot_general x8, matrix products, add_piece(): jnp.einsum('smr,mx->srx', weighted, column_hot, precision=lax.Precision.H...  24.1 us
    gather x1, local copies, waits for them, and re-layouts, local(): wanted = jnp.where(valid, jnp.take(voxel_local, source), 0)  23 us
    gather x1, local copies, waits for them, and re-layouts, local(): rates = jnp.where(valid, jnp.take(uptake_rate, source), 0.0)  23 us
    reduce_sum x1, other arithmetic, block_force(): return jnp.sum(offset * weight[None], axis=(3, 4))  15 us
  transfers between devices with their start and end apart: 24, of which 14 were waited for; matrix products, arithmetic and copies ran while one was open for 7% of the time, Pallas kernels for 0%

commit v1 on v0

v1 whole, which is shorter than its diff:
```python
import functools

import jax
import jax.numpy as jnp
from jax import lax
from jax.experimental import pallas as pl
from jax.experimental.pallas import tpu as pltpu
from jax.sharding import PartitionSpec as P

HB = 4
K = 8
ITERS = 4

MICHAELIS_HALF = 0.5
HYPOXIA_HALF = 0.6
SECRETION = 0.4
STEP_TIME = 0.5
DIFFUSION = (0.16, 0.12)
DECAY = (0.0, 0.03)
REPULSION = 1.0
ADHESION = 0.35
FORCE_SCALE = 0.08
CHEMOTAXIS = 1.5

VMEM = pl.BlockSpec(memory_space=pltpu.VMEM)
SMEM = pl.BlockSpec(memory_space=pltpu.SMEM)
LIMIT = pltpu.CompilerParams(vmem_limit_bytes=48 * 1024 * 1024)


def neighbours(block, axis, dim, width):
    count = lax.axis_size(axis)
    forward = [(i, i + 1) for i in range(count - 1)]
    backward = [(target, source) for source, target in forward]
    low = lax.ppermute(
        lax.slice_in_dim(block, block.shape[dim] - width, None, axis=dim), axis, forward
    )
    high = lax.ppermute(lax.slice_in_dim(block, 0, width, axis=dim), axis, backward)
    return low, high


def hot(index, length):
    return lax.broadcasted_iota(jnp.int32, (length, index.shape[1]), 0) == index


def halves(values):
    high = values.astype(jnp.bfloat16)
    low = (values - high.astype(jnp.float32)).astype(jnp.bfloat16)
    return high, low


def dot(a, b, contract):
    return lax.dot_general(
        a, b, ((contract[:1], contract[1:]), ((), ())), preferred_element_type=jnp.float32
    )


def pack_kernel(tiles, slot, sends, cells, out):
    width = slot + 128
    lane = lax.broadcasted_iota(jnp.int32, (2, slot), 1)
    start = jnp.int32(0)
    for d in range(tiles):
        n = sends[0, d]
        base = pl.multiple_of((start >> 7) << 7, 128)
        window = cells[:, pl.ds(base, width)]
        moved = pltpu.roll(window, width - (start - base), 1)
        out[d] = jnp.where(lane < n, moved[:2, :slot], 0.0)
        start = start + n


def unpack_kernel(tiles, slot, sends, back, force, out, padded, total):
    width = slot + 128
    capacity = out.shape[1]
    padded[...] = jnp.zeros_like(padded)
    total[...] = jnp.zeros_like(total)
    lane = lax.broadcasted_iota(jnp.int32, (8, width), 1)
    start = jnp.int32(0)
    for d in range(tiles):
        n = sends[0, d]
        base = pl.multiple_of((start >> 7) << 7, 128)
        shift = start - base
        padded[0:3, 0:slot] = back[d]
        moved = pltpu.roll(padded[...], shift, 1)
        there = jnp.logical_and(lane >= shift, lane < shift + n)
        total[:, pl.ds(base, width)] += jnp.where(there, moved, 0.0)
        start = start + n
    out[...] = FORCE_SCALE * force[0:3] + CHEMOTAXIS * total[0:3, 0:capacity]


def force_kernel(chosen, table, out, wide):
    extended = table.shape[0]

    def spread(e, carry):
        turned = jnp.transpose(table[e])
        for c in range(4):
            wide[e, c] = jnp.broadcast_to(turned[:, c : c + 1], (128, 128))
        return carry

    lax.fori_loop(0, extended, spread, 0)

    def one_block(b, carry):
        mine = table[b + HB]
        at = [jnp.broadcast_to(mine[c : c + 1], (8, 128)) for c in range(3)]

        def one_neighbour(k, sums):
            e = chosen[b, k]
            sx, sy, sz = sums
            for g in range(16):
                rows = slice(8 * g, 8 * g + 8)
                dx = at[0] - wide[e, 0, rows]
                dy = at[1] - wide[e, 1, rows]
                dz = at[2] - wide[e, 2, rows]
                far = jnp.exp(-0.25 * (dx * dx + dy * dy + dz * dz))
                square = far * far
                w = wide[e, 3, rows] * (REPULSION * (square * square) - ADHESION * far)
                sx = sx + w * dx
                sy = sy + w * dy
                sz = sz + w * dz
            return sx, sy, sz

        zero = jnp.zeros((8, 128), jnp.float32)
        sums = lax.fori_loop(0, K, one_neighbour, (zero, zero, zero))
        columns = pl.ds(pl.multiple_of(b * 128, 128), 128)
        for c in range(3):
            out[c : c + 1, columns] = mine[3:4] * jnp.sum(sums[c], axis=0, keepdims=True)
        return carry

    lax.fori_loop(0, out.shape[1] // 128, one_block, 0)


def deposit_kernel(got, field, out, oxygen):
    tiles = got.shape[0]
    planes, columns = field.shape[1:]
    out[...] = field[...]
    high, low = halves(field[0])
    oxygen[0:planes] = high
    oxygen[planes:] = low

    def one_source(t, carry):
        wanted = got[t, 0:1].astype(jnp.int32)
        given = got[t, 1:2]
        row_hot = hot(wanted // columns, planes)
        column_hot = hot(wanted % columns, columns).astype(jnp.bfloat16)
        picked = dot(oxygen[...], column_hot, (1, 0))
        picked = picked[:planes] + picked[planes:]
        o = jnp.sum(jnp.where(row_hot, picked, 0.0), axis=0, keepdims=True)
        consume = given * o / (MICHAELIS_HALF + o)
        secrete = SECRETION * given * HYPOXIA_HALF / (HYPOXIA_HALF + o)
        for s, amount in enumerate((-STEP_TIME * consume, STEP_TIME * secrete)):
            high, low = halves(jnp.where(row_hot, amount, 0.0))
            out[s] += dot(high, column_hot, (1, 1)) + dot(low, column_hot, (1, 1))
        return carry

    lax.fori_loop(0, tiles, one_source, 0)


def slope_kernel(depth, rows, got, vegf, z_low, z_high, y_low, y_high, out, near):
    tiles = got.shape[0]
    planes, columns = vegf.shape
    count = planes + 2 * rows + 2 * depth
    first = 0
    for part in (z_low, vegf, z_high, y_low, y_high):
        high, low = halves(part[...])
        near[first : first + part.shape[0]] = high
        near[count + first : count + first + part.shape[0]] = low
        first += part.shape[0]

    def one_source(t, carry):
        wanted = got[t, 0:1].astype(jnp.int32)
        row, column = wanted // columns, wanted % columns
        z, y = row // rows, row % rows
        inner = hot(column, columns).astype(jnp.bfloat16)
        values = dot(near[...], inner, (1, 0))
        values = values[:count] + values[count:]

        def at(index):
            return jnp.sum(jnp.where(hot(index, count), values, 0.0), axis=0, keepdims=True)

        below = jnp.where(y == 0, planes + 2 * rows + z, row + rows - 1)
        above = jnp.where(y == rows - 1, planes + 2 * rows + depth + z, row + rows + 1)
        out[t, 0:1] = 0.5 * (at(row + 2 * rows) - at(row))
        out[t, 1:2] = 0.5 * (at(above) - at(below))
        right = jnp.where(hot(column + 1, columns), 1.0, 0.0)
        beside = jnp.where(hot(column - 1, columns), -1.0, right).astype(jnp.bfloat16)
        change = dot(near[rows : rows + planes], beside, (1, 0))
        change = change + dot(near[count + rows : count + rows + planes], beside, (1, 0))
        change = jnp.where(hot(row, planes), change, 0.0)
        out[t, 2:3] = 0.5 * jnp.sum(change, axis=0, keepdims=True)
        return carry

    lax.fori_loop(0, tiles, one_source, 0)


def relax(center, z_low, z_high, y_low, y_high):
    along_z = jnp.concatenate([z_low, center, z_high], axis=1)
    along_y = jnp.concatenate([y_low, center, y_high], axis=2)
    along_x = jnp.pad(center, ((0, 0), (0, 0), (0, 0), (1, 1)))
    around = along_z[:, 2:] + along_z[:, :-2] + along_y[:, :, 2:] + along_y[:, :, :-2]
    around = around + along_x[..., 2:] + along_x[..., :-2]
    spread = jnp.array(DIFFUSION, jnp.float32)[:, None, None, None]
    losses = jnp.array(DECAY, jnp.float32)[:, None, None, None]
    return center + spread * (around - 6.0 * center) - losses * center


def shape_of(*shape):
    return jax.ShapeDtypeStruct(shape, jnp.float32)


def local(
    positions, radius, uptake_rate, voxel_local, cell_counts, send_counts, neighbor_blocks, field
):
    tiles = lax.axis_size("tile")
    capacity = positions.shape[1]
    slot = 2 * capacity // tiles
    blocks = capacity // 128
    species, depth, rows, columns = field.shape
    planes = depth * rows

    cells = jnp.stack([voxel_local.astype(jnp.float32), uptake_rate])
    cells = jnp.pad(cells, ((0, 6), (0, slot + 128)))
    packed = pl.pallas_call(
        functools.partial(pack_kernel, tiles, slot),
        out_shape=shape_of(tiles, 2, slot),
        in_specs=[SMEM, VMEM],
        out_specs=VMEM,
        compiler_params=LIMIT,
    )(send_counts, cells)
    got = lax.all_to_all(packed, "tile", split_axis=0, concat_axis=0, tiled=True)

    cell = jnp.arange(capacity, dtype=jnp.int32)
    kept = jnp.where(cell < cell_counts[0], radius, 0.0)
    table = jnp.concatenate([positions, kept[None]], axis=0)
    low, high = neighbours(table, "tile", 1, HB * 128)
    extended = jnp.concatenate([low, table, high], axis=1)
    extended = extended.reshape(4, blocks + 2 * HB, 128).transpose(1, 0, 2)
    extended = jnp.pad(extended, ((0, 0), (0, 4), (0, 0)))
    force = pl.pallas_call(
        force_kernel,
        out_shape=shape_of(8, capacity),
        in_specs=[SMEM, VMEM],
        out_specs=VMEM,
        scratch_shapes=[pltpu.VMEM((blocks + 2 * HB, 4, 128, 128), jnp.float32)],
        compiler_params=LIMIT,
        cost_estimate=pl.CostEstimate(
            flops=20 * capacity * K * 128, bytes_accessed=1 << 19, transcendentals=capacity * K * 128
        ),
    )(neighbor_blocks, extended)

    state = pl.pallas_call(
        deposit_kernel,
        out_shape=shape_of(species, planes, columns),
        in_specs=[VMEM, VMEM],
        out_specs=VMEM,
        scratch_shapes=[pltpu.VMEM((2 * planes, columns), jnp.bfloat16)],
        compiler_params=LIMIT,
    )(got, field.reshape(species, planes, columns))
    state = state.reshape(field.shape)
    for step in range(ITERS):
        state = relax(state, *neighbours(state, "slab", 1, 1), *neighbours(state, "tile", 2, 1))

    vegf = state[1]
    z_low, z_high = neighbours(vegf, "slab", 0, 1)
    y_low, y_high = neighbours(vegf, "tile", 1, 1)
    slopes = pl.pallas_call(
        functools.partial(slope_kernel, depth, rows),
        out_shape=shape_of(tiles, 3, slot),
        in_specs=[VMEM] * 6,
        out_specs=VMEM,
        scratch_shapes=[
            pltpu.VMEM((2 * (planes + 2 * rows + 2 * depth), columns), jnp.bfloat16)
        ],
        compiler_params=LIMIT,
    )(
        got,
        vegf.reshape(planes, columns),
        z_low.reshape(rows, columns),
        z_high.reshape(rows, columns),
        y_low.reshape(depth, columns),
        y_high.reshape(depth, columns),
    )
    back = lax.all_to_all(slopes, "tile", split_axis=0, concat_axis=0, tiled=True)
    velocity = pl.pallas_call(
        functools.partial(unpack_kernel, tiles, slot),
        out_shape=shape_of(3, capacity),
        in_specs=[SMEM, VMEM, VMEM],
        out_specs=VMEM,
        scratch_shapes=[
            pltpu.VMEM((8, slot + 128), jnp.float32),
            pltpu.VMEM((8, capacity + slot + 128), jnp.float32),
        ],
        compiler_params=LIMIT,
    )(send_counts, back, force)
    return (velocity, state)


def solution(mesh):
    placed = (
        P(None, ("slab", "tile")),
        P(("slab", "tile")),
        P(("slab", "tile")),
        P(("slab", "tile")),
        P(("slab", "tile")),
        P(("slab", "tile"), None),
        P(("slab", "tile"), None),
        P(None, "slab", "tile", None),
    )
    return jax.shard_map(
        local,
        mesh=mesh,
        in_specs=placed,
        out_specs=(P(None, ("slab", "tile")), P(None, "slab", "tile", None)),
        check_vma=False,
    )
```

time: 368 us -> 189 us (0.51)
  matrix products: 69.6 us -> 0 us
  Pallas kernels: 0 us -> 63.9 us
  starting transfers between devices: 128 us -> 64.6 us
  local copies, waits for them, and re-layouts: 66 us -> 11.5 us
  waiting for transfers between devices: 57.4 us -> 20.3 us
  other arithmetic: 41.5 us -> 12.1 us
  blocking collectives: 0 us -> 13.7 us
    dot_general x24 -> x0, matrix products: 69.6 us -> none  [the longest x16 45.5 us: one_piece(): jnp.einsum('srx,mx->srm', fields, column_hot, precision=lax.Precision.HIG...]
    pallas_call x0 -> x5, Pallas kernels: none -> 63.9 us  [the longest x1 28.5 us: local(): pl.pallas_call(deposit_kernel, out_shape=shape_of(species, planes, column...]
    all_to_all x2 -> x1, starting transfers between devices: 67.7 us -> 5.9 us  [local(): lax.all_to_all(slopes, 'tile', split_axis=0, concat_axis=0, tiled=True)]
    gather x4 -> x0, local copies, waits for them, and re-layouts: 54.2 us -> none  [the longest x1 23 us: local(): wanted = jnp.where(valid, jnp.take(voxel_local, source), 0)]
    ppermute x22, waiting for transfers between devices: 44.1 us -> 20.3 us  [the longest x11 13.3 us: neighbours(): lax.ppermute(lax.slice_in_dim(block, block.shape[dim] - width, None, axis...]
    reduce_sum x4 -> x0, other arithmetic: 17.3 us -> none  [the longest x1 15 us: block_force(): return jnp.sum(offset * weight[None], axis=(3, 4))]
    all_to_all x0 -> x1, blocking collectives: none -> 13.7 us  [local(): lax.all_to_all(packed, 'tile', split_axis=0, concat_axis=0, tiled=True)]
    all_to_all x2 -> x1, waiting for transfers between devices: 13.3 us -> 0.01 us  [local(): lax.all_to_all(slopes, 'tile', split_axis=0, concat_axis=0, tiled=True)]
  transfers between devices with their start and end apart: 24 -> 23, of which waited for: 14 -> 8; matrix products, arithmetic and copies ran while one was open for 7% -> 3% of each run, Pallas kernels for 0% -> 18%
where the time goes in v1:
time: 189 us; the launch traced here: 188 us
  starting transfers between devices  64.6 us (34%)
  Pallas kernels  63.9 us (34%)
  waiting for transfers between devices  20.3 us (11%)
  blocking collectives  13.7 us (7%)
  other arithmetic  12.1 us (6%)
  local copies, waits for them, and re-layouts  11.5 us (6%)
    ppermute x11, starting transfers between devices, neighbours(): lax.ppermute(lax.slice_in_dim(block, block.shape[dim] - width, None, axis...  44.3 us
    pallas_call x1, Pallas kernels, local(): pl.pallas_call(deposit_kernel, out_shape=shape_of(species, planes, column...  28.5 us
    pallas_call x1, Pallas kernels, local(): pl.pallas_call(functools.partial(slope_kernel, depth, rows), out_shape=sh...  18.9 us
    pallas_call x1, Pallas kernels, local(): pl.pallas_call(force_kernel, out_shape=shape_of(8, capacity), in_specs=[S...  14.5 us
    ppermute x11, starting transfers between devices, neighbours(): lax.ppermute(lax.slice_in_dim(block, 0, width, axis=dim), axis, backward)  14.4 us
    all_to_all x1, blocking collectives, local(): lax.all_to_all(packed, 'tile', split_axis=0, concat_axis=0, tiled=True)  13.7 us
    ppermute x11, waiting for transfers between devices, neighbours(): lax.ppermute(lax.slice_in_dim(block, block.shape[dim] - width, None, axis...  13.3 us
    sub x4, other arithmetic, relax(): return center + spread * (around - 6.0 * center) - losses * center  9.36 us
  transfers between devices with their start and end apart: 23, of which 8 were waited for; matrix products, arithmetic and copies ran while one was open for 3% of the time, Pallas kernels for 18%

profile of v1, /device:TPU:0, one launch (start us, length us, event | category | flops | bytes accessed | tf_op | source)
XLA Modules:
  0.0 187.9 jit_solution(7297070298942909850)
XLA Ops:
  0.6 0.7 convert_element_type.12
  1.3 0.7 select_maximum_fusion.cells
  3.4 13.7 %all_to_all.10.got = f32[8,2,512]{2,1,0:T(2,128)S(1)} all-to-all(f32[8,2,512]{2,1,0:T(2,128)S(1)} %shard_map.167), channel_id=1, replica_groups=mesh['slab'=4,'tile'=8] {'tile'}, dimensions={0} | all-to-all | bytes 65536 | tf_op jit(solution)/shard_map/all_to_all | solution.py:227
  17.1 1.6 copy-done
  18.7 28.5 %shard_map.168 = f32[2,128,2048]{2,1,0:T(8,128)S(1)} custom-call(f32[8,2,512]{2,1,0:T(2,128)S(1)} %all_to_all.10.got, f32[2,128,2048]{2,1,0:T(8,128)S(1)} %bitcast.28), custom_call_target="tpu_custom_call" | custom-call | tf_op jit(solution)/shard_map/pallas_call | solution.py:248
  47.2 1.2 copy.30
  48.8 1.3 collective-permute-start
  50.1 3.0 %collective-permute-start.1 = (f32[2,1,16,2048]{3,1,2,0:T(1,128)S(1)}, f32[2,1,16,2048]{3,1,2,0:T(1,128)S(1)}, u32[]{:S(2)}, u32[]{:S(2)}) collective-permute-start(f32[2,1,16,2048]{3,1,2,0:T(1,128)S(1)} %get-tuple-element.23), channel_id=1, source_target_pairs={{0,8},{8,16},{16,24},{1,9},{9,17},{17,25},{2,10},{10,18},{18,26},{... | collective-permute-start | bytes 786440 | tf_op jit(solution)/shard_map/ppermute | solution.py:34
  53.2 1.3 collective-permute-start.2
  54.5 4.6 %collective-permute-start.3 = (f32[2,8,1,2048]{3,1,2,0:T(8,128)S(1)}, f32[2,8,1,2048]{3,1,2,0:T(8,128)S(1)}, u32[]{:S(2)}, u32[]{:S(2)}) collective-permute-start(f32[2,8,1,2048]{3,1,2,0:T(8,128)S(1)} %get-tuple-element.25), channel_id=1, source_target_pairs={{0,1},{1,2},{2,3},{3,4},{4,5},{5,6},{6,7},{8,9},{9,10},{10,11},{11... | collective-permute-start | bytes 393224 | tf_op jit(solution)/shard_map/ppermute | solution.py:34
  59.0 2.2 %collective-permute-done.2 = f32[2,8,1,2048]{3,1,2,0:T(8,128)S(1)} collective-permute-done((f32[2,8,1,2048]{3,1,2,0:T(8,128)S(1)}, f32[2,8,1,2048]{3,1,2,0:T(8,128)S(1)}, u32[]{:S(2)}, u32[]{:S(2)}) %collective-permute-start.2) | collective-permute-done | bytes 131104 | tf_op jit(solution)/shard_map/ppermute | solution.py:37
  61.3 1.9 collective-permute-done.3
  63.2 2.3 %fusion.5 = f32[2,8,16,2048]{3,1,2,0:T(8,128)S(1)} fusion(f32[2,8,16,2048]{3,1,2,0:T(8,128)S(1)} %copy.30, f32[2,8,1,2048]{3,1,2,0:T(8,128)S(1)} %collective-permute-done.3, f32[2,8,1,2048]{3,1,2,0:T(8,128)S(1)} %collective-permute-done.2, f32[2,1,16,2048]{3,1,2,0:T(1,128)S(1)} %collective-permute-done.1, f32[2,1,16,2048]{3,1,2,0:T(1,128)S(1)} %collective-permute-done, ...), kind=kLoop, calls=%fused_computation.13 | loop fusion | flops 7864320 | bytes 4980752 | tf_op jit(solution)/shard_map/sub | solution.py:201
  65.9 1.3 collective-permute-start.4
  67.2 3.0 %collective-permute-start.5 = (f32[2,1,16,2048]{3,1,2,0:T(1,128)S(1)}, f32[2,1,16,2048]{3,1,2,0:T(1,128)S(1)}, u32[]{:S(2)}, u32[]{:S(2)}) collective-permute-start(f32[2,1,16,2048]{3,1,2,0:T(1,128)S(1)} %get-tuple-element.19), channel_id=1, source_target_pairs={{0,8},{8,16},{16,24},{1,9},{9,17},{17,25},{2,10},{10,18},{18,26},{... | collective-permute-start | bytes 786440 | tf_op jit(solution)/shard_map/ppermute | solution.py:34
  70.3 1.3 collective-permute-start.6
  71.6 5.0 %collective-permute-start.7 = (f32[2,8,1,2048]{3,1,2,0:T(8,128)S(1)}, f32[2,8,1,2048]{3,1,2,0:T(8,128)S(1)}, u32[]{:S(2)}, u32[]{:S(2)}) collective-permute-start(f32[2,8,1,2048]{3,1,2,0:T(8,128)S(1)} %get-tuple-element.21), channel_id=1, source_target_pairs={{0,1},{1,2},{2,3},{3,4},{4,5},{5,6},{6,7},{8,9},{9,10},{10,11},{11... | collective-permute-start | bytes 393224 | tf_op jit(solution)/shard_map/ppermute | solution.py:34
  76.6 1.8 collective-permute-done.6
  78.4 3.8 %collective-permute-done.7 = f32[2,8,1,2048]{3,1,2,0:T(8,128)S(1)} collective-permute-done((f32[2,8,1,2048]{3,1,2,0:T(8,128)S(1)}, f32[2,8,1,2048]{3,1,2,0:T(8,128)S(1)}, u32[]{:S(2)}, u32[]{:S(2)}) %collective-permute-start.7) | collective-permute-done | bytes 131104 | tf_op jit(solution)/shard_map/ppermute | solution.py:34
  82.2 2.3 %fusion.11 = f32[2,8,16,2048]{3,1,2,0:T(8,128)S(1)} fusion(f32[2,8,16,2048]{3,1,2,0:T(8,128)S(1)} %fusion.5, f32[2,8,1,2048]{3,1,2,0:T(8,128)S(1)} %collective-permute-done.7, f32[2,8,1,2048]{3,1,2,0:T(8,128)S(1)} %collective-permute-done.6, f32[2,1,16,2048]{3,1,2,0:T(1,128)S(1)} %collective-permute-done.5, ...), kind=kLoop, calls=%fused_computation.19 | loop fusion | flops 7864320 | bytes 4980752 | tf_op jit(solution)/shard_map/sub | solution.py:201
  84.9 1.3 collective-permute-start.8
  86.2 3.0 %collective-permute-start.9 = (f32[2,1,16,2048]{3,1,2,0:T(1,128)S(1)}, f32[2,1,16,2048]{3,1,2,0:T(1,128)S(1)}, u32[]{:S(2)}, u32[]{:S(2)}) collective-permute-start(f32[2,1,16,2048]{3,1,2,0:T(1,128)S(1)} %get-tuple-element.15), channel_id=1, source_target_pairs={{0,8},{8,16},{16,24},{1,9},{9,17},{17,25},{2,10},{10,18},{18,26},{... | collective-permute-start | bytes 786440 | tf_op jit(solution)/shard_map/ppermute | solution.py:34
  89.3 1.3 collective-permute-start.10
  90.6 5.0 %collective-permute-start.11 = (f32[2,8,1,2048]{3,1,2,0:T(8,128)S(1)}, f32[2,8,1,2048]{3,1,2,0:T(8,128)S(1)}, u32[]{:S(2)}, u32[]{:S(2)}) collective-permute-start(f32[2,8,1,2048]{3,1,2,0:T(8,128)S(1)} %get-tuple-element.17), channel_id=1, source_target_pairs={{0,1},{1,2},{2,3},{3,4},{4,5},{5,6},{6,7},{8,9},{9,10},{10,11},{11... | collective-permute-start | bytes 393224 | tf_op jit(solution)/shard_map/ppermute | solution.py:34
  96.2 1.1 collective-permute-done.10
  97.4 3.8 %collective-permute-done.11 = f32[2,8,1,2048]{3,1,2,0:T(8,128)S(1)} collective-permute-done((f32[2,8,1,2048]{3,1,2,0:T(8,128)S(1)}, f32[2,8,1,2048]{3,1,2,0:T(8,128)S(1)}, u32[]{:S(2)}, u32[]{:S(2)}) %collective-permute-start.11) | collective-permute-done | bytes 131104 | tf_op jit(solution)/shard_map/ppermute | solution.py:34
  101.2 2.4 %fusion.17 = f32[2,8,16,2048]{3,1,2,0:T(8,128)S(1)} fusion(f32[2,8,16,2048]{3,1,2,0:T(8,128)S(1)} %fusion.11, f32[2,8,1,2048]{3,1,2,0:T(8,128)S(1)} %collective-permute-done.11, f32[2,8,1,2048]{3,1,2,0:T(8,128)S(1)} %collective-permute-done.10, f32[2,1,16,2048]{3,1,2,0:T(1,128)S(1)} %collective-permute-done.9, ...), kind=kLoop, calls=%fused_computation.25 | loop fusion | flops 7864320 | bytes 4980752 | tf_op jit(solution)/shard_map/sub | solution.py:201
  103.9 1.3 collective-permute-start.12
  105.2 3.0 %collective-permute-start.13 = (f32[2,1,16,2048]{3,1,2,0:T(1,128)S(1)}, f32[2,1,16,2048]{3,1,2,0:T(1,128)S(1)}, u32[]{:S(2)}, u32[]{:S(2)}) collective-permute-start(f32[2,1,16,2048]{3,1,2,0:T(1,128)S(1)} %get-tuple-element.11), channel_id=1, source_target_pairs={{0,8},{8,16},{16,24},{1,9},{9,17},{17,25},{2,10},{10,18},{18,26},{... | collective-permute-start | bytes 786440 | tf_op jit(solution)/shard_map/ppermute | solution.py:34
  108.3 1.3 collective-permute-start.14
  109.6 5.0 %collective-permute-start.15 = (f32[2,8,1,2048]{3,1,2,0:T(8,128)S(1)}, f32[2,8,1,2048]{3,1,2,0:T(8,128)S(1)}, u32[]{:S(2)}, u32[]{:S(2)}) collective-permute-start(f32[2,8,1,2048]{3,1,2,0:T(8,128)S(1)} %get-tuple-element.13), channel_id=1, source_target_pairs={{0,1},{1,2},{2,3},{3,4},{4,5},{5,6},{6,7},{8,9},{9,10},{10,11},{11... | collective-permute-start | bytes 393224 | tf_op jit(solution)/shard_map/ppermute | solution.py:34
  114.7 1.8 collective-permute-done.14
  116.5 3.8 %collective-permute-done.15 = f32[2,8,1,2048]{3,1,2,0:T(8,128)S(1)} collective-permute-done((f32[2,8,1,2048]{3,1,2,0:T(8,128)S(1)}, f32[2,8,1,2048]{3,1,2,0:T(8,128)S(1)}, u32[]{:S(2)}, u32[]{:S(2)}) %collective-permute-start.15) | collective-permute-done | bytes 131104 | tf_op jit(solution)/shard_map/ppermute | solution.py:34
  120.3 2.3 %fusion.23 = f32[2,8,16,2048]{3,1,2,0:T(8,128)S(1)} fusion(f32[2,8,16,2048]{3,1,2,0:T(8,128)S(1)} %fusion.17, f32[2,8,1,2048]{3,1,2,0:T(8,128)S(1)} %collective-permute-done.15, f32[2,8,1,2048]{3,1,2,0:T(8,128)S(1)} %collective-permute-done.14, f32[2,1,16,2048]{3,1,2,0:T(1,128)S(1)} %collective-permute-done.13, ...), kind=kLoop, calls=%fused_computation.31 | loop fusion | flops 7864320 | bytes 4980752 | tf_op jit(solution)/shard_map/sub | solution.py:201
  122.8 0.8 slice_bitcast_fusion
  123.6 1.3 collective-permute-start.17
  124.9 3.0 %collective-permute-start.16 = (f32[1,16,2048]{2,0,1:T(1,128)}, f32[1,16,2048]{2,0,1:T(1,128)S(1)}, u32[]{:S(2)}, u32[]{:S(2)}) collective-permute-start(f32[1,16,2048]{2,0,1:T(1,128)} %get-tuple-element.9), channel_id=1, source_target_pairs={{0,8},{8,16},{16,24},{1,9},{9,17},{17,25},{2,10},{10,18},{18,26},{... | collective-permute-start | bytes 393224 | tf_op jit(solution)/shard_map/ppermute | solution.py:34
  128.5 4.4 %collective-permute-start.18 = (f32[8,1,2048]{2,0,1:T(8,128)}, f32[8,1,2048]{2,0,1:T(8,128)S(1)}, u32[]{:S(2)}, u32[]{:S(2)}) collective-permute-start(f32[8,1,2048]{2,0,1:T(8,128)} %get-tuple-element.27), channel_id=1, source_target_pairs={{0,1},{1,2},{2,3},{3,4},{4,5},{5,6},{6,7},{8,9},{9,10},{10,11},{11... | collective-permute-start | bytes 196616 | tf_op jit(solution)/shard_map/ppermute | solution.py:34
  132.9 1.3 collective-permute-start.19
  134.8 5.1 %collective-permute-start.20 = (f32[4,512]{1,0:T(4,128)}, f32[4,512]{1,0:T(4,128)}, u32[]{:S(2)}, u32[]{:S(2)}) collective-permute-start(f32[4,512]{1,0:T(4,128)} %get-tuple-element.28), channel_id=1, source_target_pairs={{0,1},{1,2},{2,3},{3,4},{4,5},{5,6},{6,7},{8,9},{9,10},{10,11},{11... | collective-permute-start | bytes 24584 | tf_op jit(solution)/shard_map/ppermute | solution.py:34
  140.6 1.5 collective-permute-start.21
  142.1 0.8 copy.33.chosen
  143.9 18.9 %shard_map.169 = f32[8,3,512]{2,1,0:T(4,128)} custom-call(f32[8,2,512]{2,1,0:T(2,128)S(1)} %all_to_all.10.got, f32[128,2048]{1,0:T(8,128)S(1)} %bitcast.27, f32[16,2048]{1,0:T(8,128)S(1)} %bitcast.30, f32[16,2048]{1,0:T(8,128)S(1)} %bitcast.29, f32[8,2048]{1,0:T(8,128)S(1)} %bitcast.31, f32[8,2048]{1,0:T(8,128)S(1)} %bitcast.32), custom_call_target="tpu_custom_call" | custom-call | tf_op jit(solution)/shard_map/pallas_call | solution.py:263
  162.8 5.9 %all-to-all-start.1 = ((f32[8,3,512]{2,1,0:T(4,128)}), f32[8,3,512]{2,1,0:T(4,128)S(1)}, u32[]{:S(2)}, u32[]{:S(2)}) async-start(f32[8,3,512]{2,1,0:T(4,128)} %shard_map.169), calls=%async_computation.1 | async-start | bytes 131072 | tf_op jit(solution)/shard_map/all_to_all | solution.py:280
  168.7 0.7 maximum_bitcast_fusion
  169.5 14.5 %shard_map.170.force = f32[8,2048]{1,0:T(8,128)S(1)} custom-call(s32[16,8]{1,0:T(8,128)S(1)} %copy.33.chosen, f32[24,8,128]{2,1,0:T(8,128)S(1)} %pad.26.table), custom_call_target="tpu_custom_call" | custom-call | flops 41943040 | bytes 524288 | tf_op jit(solution)/shard_map/pallas_call | solution.py:236
  184.0 2.5 %copy.34 = f32[2,8,16,2048]{3,2,1,0:T(8,128)} copy(f32[2,8,16,2048]{3,1,2,0:T(8,128)S(1)} %fusion.23) | data formatting | bytes 4194304
  186.6 1.3 shard_map.171
  (49 shorter events, 5.9 us)
Async XLA Ops:
  2.1 0.7 copy-start.1
  17.1 1.6 copy-start
  47.2 16.0 %copy-start.7 = (f32[2]{0:T(128)S(1)}, f32[2]{0:T(128)}, u32[]{:S(2)}) copy-start(f32[2]{0:T(128)} %constant.10.clone) | copy-start | bytes 28
  47.2 16.0 %copy-start.8 = (f32[2]{0:T(128)S(1)}, f32[2]{0:T(128)}, u32[]{:S(2)}) copy-start(f32[2]{0:T(128)} %constant.11.clone) | copy-start | bytes 28
  48.8 14.4 %collective-permute-start = (f32[2,1,16,2048]{3,1,2,0:T(1,128)S(1)}, f32[2,1,16,2048]{3,1,2,0:T(1,128)S(1)}, u32[]{:S(2)}, u32[]{:S(2)}) collective-permute-start(f32[2,1,16,2048]{3,1,2,0:T(1,128)S(1)} %get-tuple-element.22), channel_id=1, source_target_pairs={{8,0},{16,8},{24,16},{9,1},{17,9},{25,17},{10,2},{18,10},{26,18},{... | collective-permute-start | bytes 786440 | tf_op jit(solution)/shard_map/ppermute | solution.py:37
  50.1 13.1 %collective-permute-start.1 = (f32[2,1,16,2048]{3,1,2,0:T(1,128)S(1)}, f32[2,1,16,2048]{3,1,2,0:T(1,128)S(1)}, u32[]{:S(2)}, u32[]{:S(2)}) collective-permute-start(f32[2,1,16,2048]{3,1,2,0:T(1,128)S(1)} %get-tuple-element.23), channel_id=1, source_target_pairs={{0,8},{8,16},{16,24},{1,9},{9,17},{17,25},{2,10},{10,18},{18,26},{... | collective-permute-start | bytes 786440 | tf_op jit(solution)/shard_map/ppermute | solution.py:34
  53.2 8.1 %collective-permute-start.2 = (f32[2,8,1,2048]{3,1,2,0:T(8,128)S(1)}, f32[2,8,1,2048]{3,1,2,0:T(8,128)S(1)}, u32[]{:S(2)}, u32[]{:S(2)}) collective-permute-start(f32[2,8,1,2048]{3,1,2,0:T(8,128)S(1)} %get-tuple-element.24), channel_id=1, source_target_pairs={{1,0},{2,1},{3,2},{4,3},{5,4},{6,5},{7,6},{9,8},{10,9},{11,10},{12... | collective-permute-start | bytes 393224 | tf_op jit(solution)/shard_map/ppermute | solution.py:37
  54.5 8.7 %collective-permute-start.3 = (f32[2,8,1,2048]{3,1,2,0:T(8,128)S(1)}, f32[2,8,1,2048]{3,1,2,0:T(8,128)S(1)}, u32[]{:S(2)}, u32[]{:S(2)}) collective-permute-start(f32[2,8,1,2048]{3,1,2,0:T(8,128)S(1)} %get-tuple-element.25), channel_id=1, source_target_pairs={{0,1},{1,2},{2,3},{3,4},{4,5},{5,6},{6,7},{8,9},{9,10},{10,11},{11... | collective-permute-start | bytes 393224 | tf_op jit(solution)/shard_map/ppermute | solution.py:34
  65.9 16.3 %collective-permute-start.4 = (f32[2,1,16,2048]{3,1,2,0:T(1,128)S(1)}, f32[2,1,16,2048]{3,1,2,0:T(1,128)S(1)}, u32[]{:S(2)}, u32[]{:S(2)}) collective-permute-start(f32[2,1,16,2048]{3,1,2,0:T(1,128)S(1)} %get-tuple-element.18), channel_id=1, source_target_pairs={{8,0},{16,8},{24,16},{9,1},{17,9},{25,17},{10,2},{18,10},{26,18},{... | collective-permute-start | bytes 786440 | tf_op jit(solution)/shard_map/ppermute | solution.py:37
  67.2 15.0 %collective-permute-start.5 = (f32[2,1,16,2048]{3,1,2,0:T(1,128)S(1)}, f32[2,1,16,2048]{3,1,2,0:T(1,128)S(1)}, u32[]{:S(2)}, u32[]{:S(2)}) collective-permute-start(f32[2,1,16,2048]{3,1,2,0:T(1,128)S(1)} %get-tuple-element.19), channel_id=1, source_target_pairs={{0,8},{8,16},{16,24},{1,9},{9,17},{17,25},{2,10},{10,18},{18,26},{... | collective-permute-start | bytes 786440 | tf_op jit(solution)/shard_map/ppermute | solution.py:34
  70.3 8.1 %collective-permute-start.6 = (f32[2,8,1,2048]{3,1,2,0:T(8,128)S(1)}, f32[2,8,1,2048]{3,1,2,0:T(8,128)S(1)}, u32[]{:S(2)}, u32[]{:S(2)}) collective-permute-start(f32[2,8,1,2048]{3,1,2,0:T(8,128)S(1)} %get-tuple-element.20), channel_id=1, source_target_pairs={{1,0},{2,1},{3,2},{4,3},{5,4},{6,5},{7,6},{9,8},{10,9},{11,10},{12... | collective-permute-start | bytes 393224 | tf_op jit(solution)/shard_map/ppermute | solution.py:37
  71.6 10.6 %collective-permute-start.7 = (f32[2,8,1,2048]{3,1,2,0:T(8,128)S(1)}, f32[2,8,1,2048]{3,1,2,0:T(8,128)S(1)}, u32[]{:S(2)}, u32[]{:S(2)}) collective-permute-start(f32[2,8,1,2048]{3,1,2,0:T(8,128)S(1)} %get-tuple-element.21), channel_id=1, source_target_pairs={{0,1},{1,2},{2,3},{3,4},{4,5},{5,6},{6,7},{8,9},{9,10},{10,11},{11... | collective-permute-start | bytes 393224 | tf_op jit(solution)/shard_map/ppermute | solution.py:34
  84.9 16.3 %collective-permute-start.8 = (f32[2,1,16,2048]{3,1,2,0:T(1,128)S(1)}, f32[2,1,16,2048]{3,1,2,0:T(1,128)S(1)}, u32[]{:S(2)}, u32[]{:S(2)}) collective-permute-start(f32[2,1,16,2048]{3,1,2,0:T(1,128)S(1)} %get-tuple-element.14), channel_id=1, source_target_pairs={{8,0},{16,8},{24,16},{9,1},{17,9},{25,17},{10,2},{18,10},{26,18},{... | collective-permute-start | bytes 786440 | tf_op jit(solution)/shard_map/ppermute | solution.py:37
  86.2 15.0 %collective-permute-start.9 = (f32[2,1,16,2048]{3,1,2,0:T(1,128)S(1)}, f32[2,1,16,2048]{3,1,2,0:T(1,128)S(1)}, u32[]{:S(2)}, u32[]{:S(2)}) collective-permute-start(f32[2,1,16,2048]{3,1,2,0:T(1,128)S(1)} %get-tuple-element.15), channel_id=1, source_target_pairs={{0,8},{8,16},{16,24},{1,9},{9,17},{17,25},{2,10},{10,18},{18,26},{... | collective-permute-start | bytes 786440 | tf_op jit(solution)/shard_map/ppermute | solution.py:34
  89.3 8.1 %collective-permute-start.10 = (f32[2,8,1,2048]{3,1,2,0:T(8,128)S(1)}, f32[2,8,1,2048]{3,1,2,0:T(8,128)S(1)}, u32[]{:S(2)}, u32[]{:S(2)}) collective-permute-start(f32[2,8,1,2048]{3,1,2,0:T(8,128)S(1)} %get-tuple-element.16), channel_id=1, source_target_pairs={{1,0},{2,1},{3,2},{4,3},{5,4},{6,5},{7,6},{9,8},{10,9},{11,10},{12... | collective-permute-start | bytes 393224 | tf_op jit(solution)/shard_map/ppermute | solution.py:37
  90.6 10.6 %collective-permute-start.11 = (f32[2,8,1,2048]{3,1,2,0:T(8,128)S(1)}, f32[2,8,1,2048]{3,1,2,0:T(8,128)S(1)}, u32[]{:S(2)}, u32[]{:S(2)}) collective-permute-start(f32[2,8,1,2048]{3,1,2,0:T(8,128)S(1)} %get-tuple-element.17), channel_id=1, source_target_pairs={{0,1},{1,2},{2,3},{3,4},{4,5},{5,6},{6,7},{8,9},{9,10},{10,11},{11... | collective-permute-start | bytes 393224 | tf_op jit(solution)/shard_map/ppermute | solution.py:34
  96.2 18.4 %copy-start.6 = (f32[2048]{0:T(1024)S(1)}, f32[2048]{0:T(1024)}, u32[]{:S(2)}) copy-start(f32[2048]{0:T(1024)} %param.17) | copy-start | bytes 24580
  103.9 16.3 %collective-permute-start.12 = (f32[2,1,16,2048]{3,1,2,0:T(1,128)S(1)}, f32[2,1,16,2048]{3,1,2,0:T(1,128)S(1)}, u32[]{:S(2)}, u32[]{:S(2)}) collective-permute-start(f32[2,1,16,2048]{3,1,2,0:T(1,128)S(1)} %get-tuple-element.10), channel_id=1, source_target_pairs={{8,0},{16,8},{24,16},{9,1},{17,9},{25,17},{10,2},{18,10},{26,18},{... | collective-permute-start | bytes 786440 | tf_op jit(solution)/shard_map/ppermute | solution.py:37
  105.2 15.0 %collective-permute-start.13 = (f32[2,1,16,2048]{3,1,2,0:T(1,128)S(1)}, f32[2,1,16,2048]{3,1,2,0:T(1,128)S(1)}, u32[]{:S(2)}, u32[]{:S(2)}) collective-permute-start(f32[2,1,16,2048]{3,1,2,0:T(1,128)S(1)} %get-tuple-element.11), channel_id=1, source_target_pairs={{0,8},{8,16},{16,24},{1,9},{9,17},{17,25},{2,10},{10,18},{18,26},{... | collective-permute-start | bytes 786440 | tf_op jit(solution)/shard_map/ppermute | solution.py:34
  108.3 8.1 %collective-permute-start.14 = (f32[2,8,1,2048]{3,1,2,0:T(8,128)S(1)}, f32[2,8,1,2048]{3,1,2,0:T(8,128)S(1)}, u32[]{:S(2)}, u32[]{:S(2)}) collective-permute-start(f32[2,8,1,2048]{3,1,2,0:T(8,128)S(1)} %get-tuple-element.12), channel_id=1, source_target_pairs={{1,0},{2,1},{3,2},{4,3},{5,4},{6,5},{7,6},{9,8},{10,9},{11,10},{12... | collective-permute-start | bytes 393224 | tf_op jit(solution)/shard_map/ppermute | solution.py:37
  109.6 10.6 %collective-permute-start.15 = (f32[2,8,1,2048]{3,1,2,0:T(8,128)S(1)}, f32[2,8,1,2048]{3,1,2,0:T(8,128)S(1)}, u32[]{:S(2)}, u32[]{:S(2)}) collective-permute-start(f32[2,8,1,2048]{3,1,2,0:T(8,128)S(1)} %get-tuple-element.13), channel_id=1, source_target_pairs={{0,1},{1,2},{2,3},{3,4},{4,5},{5,6},{6,7},{8,9},{9,10},{10,11},{11... | collective-permute-start | bytes 393224 | tf_op jit(solution)/shard_map/ppermute | solution.py:34
  122.6 11.6 %copy-start.3 = (f32[3,2048]{1,0:T(4,128)S(1)}, f32[3,2048]{1,0:T(4,128)}, u32[]{:S(2)}) copy-start(f32[3,2048]{1,0:T(4,128)} %param.16) | copy-start | bytes 73732
  123.6 16.4 %collective-permute-start.17 = (f32[1,16,2048]{2,0,1:T(1,128)S(1)}, f32[1,16,2048]{2,0,1:T(1,128)S(1)}, u32[]{:S(2)}, u32[]{:S(2)}) collective-permute-start(f32[1,16,2048]{2,0,1:T(1,128)S(1)} %get-tuple-element.8), channel_id=1, source_target_pairs={{8,0},{16,8},{24,16},{9,1},{17,9},{25,17},{10,2},{18,10},{26,18},{... | collective-permute-start | bytes 393224 | tf_op jit(solution)/shard_map/ppermute | solution.py:37
  124.9 19.0 %collective-permute-start.16 = (f32[1,16,2048]{2,0,1:T(1,128)}, f32[1,16,2048]{2,0,1:T(1,128)S(1)}, u32[]{:S(2)}, u32[]{:S(2)}) collective-permute-start(f32[1,16,2048]{2,0,1:T(1,128)} %get-tuple-element.9), channel_id=1, source_target_pairs={{0,8},{8,16},{16,24},{1,9},{9,17},{17,25},{2,10},{10,18},{18,26},{... | collective-permute-start | bytes 393224 | tf_op jit(solution)/shard_map/ppermute | solution.py:34
  128.5 15.3 %collective-permute-start.18 = (f32[8,1,2048]{2,0,1:T(8,128)}, f32[8,1,2048]{2,0,1:T(8,128)S(1)}, u32[]{:S(2)}, u32[]{:S(2)}) collective-permute-start(f32[8,1,2048]{2,0,1:T(8,128)} %get-tuple-element.27), channel_id=1, source_target_pairs={{0,1},{1,2},{2,3},{3,4},{4,5},{5,6},{6,7},{8,9},{9,10},{10,11},{11... | collective-permute-start | bytes 196616 | tf_op jit(solution)/shard_map/ppermute | solution.py:34
  132.9 11.0 %collective-permute-start.19 = (f32[8,1,2048]{2,0,1:T(8,128)S(1)}, f32[8,1,2048]{2,0,1:T(8,128)S(1)}, u32[]{:S(2)}, u32[]{:S(2)}) collective-permute-start(f32[8,1,2048]{2,0,1:T(8,128)S(1)} %get-tuple-element.26), channel_id=1, source_target_pairs={{1,0},{2,1},{3,2},{4,3},{5,4},{6,5},{7,6},{9,8},{10,9},{11,10},{12... | collective-permute-start | bytes 196616 | tf_op jit(solution)/shard_map/ppermute | solution.py:37
  134.8 33.9 %collective-permute-start.20 = (f32[4,512]{1,0:T(4,128)}, f32[4,512]{1,0:T(4,128)}, u32[]{:S(2)}, u32[]{:S(2)}) collective-permute-start(f32[4,512]{1,0:T(4,128)} %get-tuple-element.28), channel_id=1, source_target_pairs={{0,1},{1,2},{2,3},{3,4},{4,5},{5,6},{6,7},{8,9},{9,10},{10,11},{11... | collective-permute-start | bytes 24584 | tf_op jit(solution)/shard_map/ppermute | solution.py:34
  140.0 0.7 copy-start.4
  140.6 28.1 %collective-permute-start.21 = (f32[4,512]{1,0:T(4,128)}, f32[4,512]{1,0:T(4,128)}, u32[]{:S(2)}, u32[]{:S(2)}) collective-permute-start(f32[4,512]{1,0:T(4,128)} %get-tuple-element.29), channel_id=1, source_target_pairs={{1,0},{2,1},{3,2},{4,3},{5,4},{6,5},{7,6},{9,8},{10,9},{11,10},{12... | collective-permute-start | bytes 24584 | tf_op jit(solution)/shard_map/ppermute | solution.py:37
  142.9 0.9 copy-start.5
  162.8 23.7 %all-to-all-start.1 = ((f32[8,3,512]{2,1,0:T(4,128)}), f32[8,3,512]{2,1,0:T(4,128)S(1)}, u32[]{:S(2)}, u32[]{:S(2)}) async-start(f32[8,3,512]{2,1,0:T(4,128)} %shard_map.169), calls=%async_computation.1 | async-start | bytes 131072 | tf_op jit(solution)/shard_map/all_to_all | solution.py:280
  184.0 2.6 %copy-start.2 = (s32[1,8]{1,0:T(1,128)S(1)}, s32[1,8]{1,0:T(1,128)}, u32[]{:S(2)}) copy-start(s32[1,8]{1,0:T(1,128)} %sends.3) | copy-start | bytes 100

commit v2 on v1

--- a/solution.py
+++ b/solution.py
@@ -27,15 +27,105 @@
 LIMIT = pltpu.CompilerParams(vmem_limit_bytes=48 * 1024 * 1024)
 
 
-def neighbours(block, axis, dim, width):
-    count = lax.axis_size(axis)
-    forward = [(i, i + 1) for i in range(count - 1)]
-    backward = [(target, source) for source, target in forward]
-    low = lax.ppermute(
-        lax.slice_in_dim(block, block.shape[dim] - width, None, axis=dim), axis, forward
-    )
-    high = lax.ppermute(lax.slice_in_dim(block, 0, width, axis=dim), axis, backward)
-    return low, high
+MESH = pl.DeviceIdType.MESH
+
+
+def swap(tiles, source, held, send_sem, recv_sem):
+    me = lax.axis_index("tile")
+    copies = []
+    for i in range(1, tiles):
+        to = lax.rem(me + i, tiles)
+        copy = pltpu.make_async_remote_copy(
+            src_ref=source.at[to],
+            dst_ref=held.at[me],
+            send_sem=send_sem.at[i],
+            recv_sem=recv_sem.at[i],
+            device_id={"tile": to},
+            device_id_type=MESH,
+        )
+        copy.start()
+        copies.append(copy)
+    return copies
+
+
+def greet(tiles):
+    me = lax.axis_index("tile")
+    barrier = pltpu.get_barrier_semaphore()
+    for i in range(1, tiles):
+        pl.semaphore_signal(
+            barrier, inc=1, device_id={"tile": lax.rem(me + i, tiles)}, device_id_type=MESH
+        )
+    pl.semaphore_wait(barrier, tiles - 1)
+
+
+def meet_kernel(tiles, packed, table, got, extended, held, sides, send_sem, recv_sem, side_sem):
+    me = lax.axis_index("tile")
+    capacity = table.shape[1]
+    width = HB * 128
+    sides[...] = jnp.zeros_like(sides)
+    greet(tiles)
+    copies = swap(tiles, packed, held, send_sem, recv_sem)
+    up = pltpu.make_async_remote_copy(
+        src_ref=table.at[:, capacity - width :],
+        dst_ref=sides.at[0],
+        send_sem=side_sem.at[0],
+        recv_sem=side_sem.at[1],
+        device_id={"tile": jnp.minimum(me + 1, tiles - 1)},
+        device_id_type=MESH,
+    )
+    down = pltpu.make_async_remote_copy(
+        src_ref=table.at[:, :width],
+        dst_ref=sides.at[1],
+        send_sem=side_sem.at[2],
+        recv_sem=side_sem.at[3],
+        device_id={"tile": jnp.maximum(me - 1, 0)},
+        device_id_type=MESH,
+    )
+
+    @pl.when(me < tiles - 1)
+    def _():
+        up.start()
+
+    @pl.when(me > 0)
+    def _():
+        down.start()
+
+    blocks = capacity // 128
+    extended[...] = jnp.zeros_like(extended)
+    for b in range(blocks):
+        extended[HB + b, 0:4] = table[:, 128 * b : 128 * b + 128]
+    got[me] = packed[me]
+
+    @pl.when(me < tiles - 1)
+    def _():
+        up.wait_send()
+        down.wait_recv()
+
+    @pl.when(me > 0)
+    def _():
+        down.wait_send()
+        up.wait_recv()
+
+    for b in range(HB):
+        extended[b, 0:4] = sides[0, :, 128 * b : 128 * b + 128]
+        extended[HB + blocks + b, 0:4] = sides[1, :, 128 * b : 128 * b + 128]
+    for copy in copies:
+        copy.wait()
+    for i in range(1, tiles):
+        other = lax.rem(me + i, tiles)
+        got[other] = held[other]
+
+
+def return_kernel(tiles, slopes, back, held, send_sem, recv_sem):
+    me = lax.axis_index("tile")
+    greet(tiles)
+    copies = swap(tiles, slopes, held, send_sem, recv_sem)
+    back[me] = slopes[me]
+    for copy in copies:
+        copy.wait()
+    for i in range(1, tiles):
+        other = lax.rem(me + i, tiles)
+        back[other] = held[other]
 
 
 def hot(index, length):
@@ -86,17 +176,17 @@
     out[...] = FORCE_SCALE * force[0:3] + CHEMOTAXIS * total[0:3, 0:capacity]
 
 
-def force_kernel(chosen, table, out, wide):
-    extended = table.shape[0]
-
-    def spread(e, carry):
+def widen(table, wide):
+    def one(e, carry):
         turned = jnp.transpose(table[e])
         for c in range(4):
             wide[e, c] = jnp.broadcast_to(turned[:, c : c + 1], (128, 128))
         return carry
 
-    lax.fori_loop(0, extended, spread, 0)
-
+    lax.fori_loop(0, table.shape[0], one, 0)
+
+
+def force_blocks(chosen, table, wide, out, first, last):
     def one_block(b, carry):
         mine = table[b + HB]
         at = [jnp.broadcast_to(mine[c : c + 1], (8, 128)) for c in range(3)]
@@ -124,7 +214,148 @@
             out[c : c + 1, columns] = mine[3:4] * jnp.sum(sums[c], axis=0, keepdims=True)
         return carry
 
-    lax.fori_loop(0, out.shape[1] // 128, one_block, 0)
+    lax.fori_loop(first, last, one_block, 0)
+
+
+def diffuse_kernel(
+    slabs,
+    tiles,
+    chosen,
+    table,
+    start,
+    out,
+    force,
+    edge_z,
+    edge_y,
+    state,
+    wide,
+    sent_y,
+    halo_z,
+    halo_y,
+    send_sem,
+    recv_sem,
+):
+    species, depth, rows, columns = start.shape
+    slab, tile = lax.axis_index("slab"), lax.axis_index("tile")
+    sides = (
+        ("slab", slab, slabs, 0),
+        ("slab", slab, slabs, 1),
+        ("tile", tile, tiles, 0),
+        ("tile", tile, tiles, 1),
+    )
+
+    def exists(side):
+        axis, at, count, up = side
+        return at < count - 1 if up else at > 0
+
+    def partner(side):
+        axis, at, count, up = side
+        return {axis: jnp.minimum(at + 1, count - 1) if up else jnp.maximum(at - 1, 0)}
+
+    halo_z[...] = jnp.zeros_like(halo_z)
+    halo_y[...] = jnp.zeros_like(halo_y)
+    barrier = pltpu.get_barrier_semaphore()
+    for side in sides:
+
+        @pl.when(exists(side))
+        def _(side=side):
+            pl.semaphore_signal(barrier, inc=1, device_id=partner(side), device_id_type=MESH)
+
+    count = sum(exists(side).astype(jnp.int32) for side in sides)
+    pl.semaphore_wait(barrier, count)
+
+    def copies(step, now, which):
+        made = []
+        for n, side in enumerate(sides):
+            up = side[3]
+            if n < 2:
+                source = state.at[now, which, depth if up else 1]
+                target = halo_z.at[step, 1 - up, which]
+            else:
+                source = sent_y.at[step, up, which]
+                target = halo_y.at[step, 1 - up, which]
+            made.append(
+                pltpu.make_async_remote_copy(
+                    src_ref=source,
+                    dst_ref=target,
+                    send_sem=send_sem.at[step, n],
+                    recv_sem=recv_sem.at[step, n],
+                    device_id=partner(side),
+                    device_id_type=MESH,
+                )
+            )
+        return made
+
+    def begin(step, now, which):
+        for up in range(2):
+            sent_y[step, up] = state[now, :, 1 : depth + 1, (rows - 1) * up, :]
+        made = copies(step, now, which)
+        for n in (2, 3, 0, 1):
+
+            @pl.when(exists(sides[n]))
+            def _(n=n):
+                made[n].start()
+
+        return made
+
+    def finish(made):
+        for n, side in enumerate(sides):
+
+            @pl.when(exists(side))
+            def _(n=n):
+                made[n].wait_send()
+                made[n ^ 1].wait_recv()
+
+    blocks = force.shape[1] // 128
+    share = blocks // (ITERS + 1)
+    for now in range(2):
+        for s in range(species):
+            for z in (0, depth + 1):
+                state[now, s, z] = jnp.zeros((rows, columns), jnp.float32)
+    state[0, :, 1 : depth + 1] = start[...]
+    lane = lax.broadcasted_iota(jnp.int32, (rows, columns), 1)
+    row = lax.broadcasted_iota(jnp.int32, (rows, columns), 0)
+
+    def one_step(step, carry):
+        now = lax.rem(step, 2)
+        later = 1 - now
+        made = begin(step, now, slice(0, species))
+
+        @pl.when(step == 0)
+        def _():
+            widen(table, wide)
+
+        for s in range(species):
+
+            def one_plane(z, carry):
+                c = state[now, s, z]
+                around = state[now, s, z - 1] + state[now, s, z + 1]
+                around += jnp.where(row == 0, 0.0, pltpu.roll(c, 1, 0))
+                around += jnp.where(row == rows - 1, 0.0, pltpu.roll(c, rows - 1, 0))
+                around += jnp.where(lane == 0, 0.0, pltpu.roll(c, 1, 1))
+                around += jnp.where(lane == columns - 1, 0.0, pltpu.roll(c, columns - 1, 1))
+                state[later, s, z] = c + DIFFUSION[s] * (around - 6.0 * c) - DECAY[s] * c
+                return carry
+
+            lax.fori_loop(1, depth + 1, one_plane, 0)
+        force_blocks(chosen, table, wide, force, step * share, (step + 1) * share)
+        finish(made)
+        for s in range(species):
+            for up in range(2):
+                state[later, s, depth if up else 1] += DIFFUSION[s] * halo_z[step, up, s]
+                for z in range(depth):
+                    edge = slice((rows - 1) * up, (rows - 1) * up + 1)
+                    state[later, s, z + 1, edge] += DIFFUSION[s] * halo_y[step, up, s, z : z + 1]
+        return carry
+
+    lax.fori_loop(0, ITERS, one_step, 0)
+    last = ITERS % 2
+    made = begin(ITERS, last, 1)
+    force_blocks(chosen, table, wide, force, ITERS * share, blocks)
+    out[...] = state[last, :, 1 : depth + 1]
+    finish(made)
+    edge_z[...] = halo_z[ITERS, :, 1]
+    edge_y[...] = halo_y[ITERS, :, 1]
 
 
 def deposit_kernel(got, field, out, oxygen):
@@ -153,13 +384,13 @@
     lax.fori_loop(0, tiles, one_source, 0)
 
 
-def slope_kernel(depth, rows, got, vegf, z_low, z_high, y_low, y_high, out, near):
+def slope_kernel(depth, rows, got, field, edge_z, edge_y, out, near):
     tiles = got.shape[0]
-    planes, columns = vegf.shape
+    planes, columns = field.shape[1:]
     count = planes + 2 * rows + 2 * depth
     first = 0
-    for part in (z_low, vegf, z_high, y_low, y_high):
-        high, low = halves(part[...])
+    for part in (edge_z[0], field[1], edge_z[1], edge_y[0], edge_y[1]):
+        high, low = halves(part)
         near[first : first + part.shape[0]] = high
         near[count + first : count + first + part.shape[0]] = low
         first += part.shape[0]
@@ -190,15 +421,10 @@
     lax.fori_loop(0, tiles, one_source, 0)
 
 
-def relax(center, z_low, z_high, y_low, y_high):
-    along_z = jnp.concatenate([z_low, center, z_high], axis=1)
-    along_y = jnp.concatenate([y_low, center, y_high], axis=2)
-    along_x = jnp.pad(center, ((0, 0), (0, 0), (0, 0), (1, 1)))
-    around = along_z[:, 2:] + along_z[:, :-2] + along_y[:, :, 2:] + along_y[:, :, :-2]
-    around = around + along_x[..., 2:] + along_x[..., :-2]
-    spread = jnp.array(DIFFUSION, jnp.float32)[:, None, None, None]
-    losses = jnp.array(DECAY, jnp.float32)[:, None, None, None]
-    return center + spread * (around - 6.0 * center) - losses * center
+def remote(number):
+    return pltpu.CompilerParams(
+        vmem_limit_bytes=48 * 1024 * 1024, collective_id=number, has_side_effects=True
+    )
 
 
 def shape_of(*shape):
@@ -208,7 +434,7 @@
 def local(
     positions, radius, uptake_rate, voxel_local, cell_counts, send_counts, neighbor_blocks, field
 ):
-    tiles = lax.axis_size("tile")
+    slabs, tiles = lax.axis_size("slab"), lax.axis_size("tile")
     capacity = positions.shape[1]
     slot = 2 * capacity // tiles
     blocks = capacity // 128
@@ -224,26 +450,23 @@
         out_specs=VMEM,
         compiler_params=LIMIT,
     )(send_counts, cells)
-    got = lax.all_to_all(packed, "tile", split_axis=0, concat_axis=0, tiled=True)
-
     cell = jnp.arange(capacity, dtype=jnp.int32)
     kept = jnp.where(cell < cell_counts[0], radius, 0.0)
     table = jnp.concatenate([positions, kept[None]], axis=0)
-    low, high = neighbours(table, "tile", 1, HB * 128)
-    extended = jnp.concatenate([low, table, high], axis=1)
-    extended = extended.reshape(4, blocks + 2 * HB, 128).transpose(1, 0, 2)
-    extended = jnp.pad(extended, ((0, 0), (0, 4), (0, 0)))
-    force = pl.pallas_call(
-        force_kernel,
-        out_shape=shape_of(8, capacity),
-        in_specs=[SMEM, VMEM],
-        out_specs=VMEM,
-        scratch_shapes=[pltpu.VMEM((blocks + 2 * HB, 4, 128, 128), jnp.float32)],
-        compiler_params=LIMIT,
-        cost_estimate=pl.CostEstimate(
-            flops=20 * capacity * K * 128, bytes_accessed=1 << 19, transcendentals=capacity * K * 128
-        ),
-    )(neighbor_blocks, extended)
+    got, extended = pl.pallas_call(
+        functools.partial(meet_kernel, tiles),
+        out_shape=(shape_of(tiles, 2, slot), shape_of(blocks + 2 * HB, 8, 128)),
+        in_specs=[VMEM, VMEM],
+        out_specs=[VMEM, VMEM],
+        scratch_shapes=[
+            pltpu.VMEM((tiles, 2, slot), jnp.float32),
+            pltpu.VMEM((2, 4, HB * 128), jnp.float32),
+            pltpu.SemaphoreType.DMA((tiles,)),
+            pltpu.SemaphoreType.DMA((tiles,)),
+            pltpu.SemaphoreType.DMA((4,)),
+        ],
+        compiler_params=remote(0),
+    )(packed, table)
 
     state = pl.pallas_call(
         deposit_kernel,
@@ -253,31 +476,51 @@
         scratch_shapes=[pltpu.VMEM((2 * planes, columns), jnp.bfloat16)],
         compiler_params=LIMIT,
     )(got, field.reshape(species, planes, columns))
-    state = state.reshape(field.shape)
-    for step in range(ITERS):
-        state = relax(state, *neighbours(state, "slab", 1, 1), *neighbours(state, "tile", 2, 1))
-
-    vegf = state[1]
-    z_low, z_high = neighbours(vegf, "slab", 0, 1)
-    y_low, y_high = neighbours(vegf, "tile", 1, 1)
+    steps = ITERS + 1
+    state, force, edge_z, edge_y = pl.pallas_call(
+        functools.partial(diffuse_kernel, slabs, tiles),
+        out_shape=(
+            shape_of(*field.shape),
+            shape_of(8, capacity),
+            shape_of(2, rows, columns),
+            shape_of(2, depth, columns),
+        ),
+        in_specs=[SMEM, VMEM, VMEM],
+        out_specs=[VMEM] * 4,
+        scratch_shapes=[
+            pltpu.VMEM((2, species, depth + 2, rows, columns), jnp.float32),
+            pltpu.VMEM((blocks + 2 * HB, 4, 128, 128), jnp.float32),
+            pltpu.VMEM((steps, 2, species, depth, columns), jnp.float32),
+            pltpu.VMEM((steps, 2, species, rows, columns), jnp.float32),
+            pltpu.VMEM((steps, 2, species, depth, columns), jnp.float32),
+            pltpu.SemaphoreType.DMA((steps, 4)),
+            pltpu.SemaphoreType.DMA((steps, 4)),
+        ],
+        compiler_params=remote(1),
+    )(neighbor_blocks, extended, state.reshape(field.shape))
+
     slopes = pl.pallas_call(
         functools.partial(slope_kernel, depth, rows),
         out_shape=shape_of(tiles, 3, slot),
-        in_specs=[VMEM] * 6,
+        in_specs=[VMEM] * 4,
         out_specs=VMEM,
         scratch_shapes=[
             pltpu.VMEM((2 * (planes + 2 * rows + 2 * depth), columns), jnp.bfloat16)
         ],
         compiler_params=LIMIT,
-    )(
-        got,
-        vegf.reshape(planes, columns),
-        z_low.reshape(rows, columns),
-        z_high.reshape(rows, columns),
-        y_low.reshape(depth, columns),
-        y_high.reshape(depth, columns),
-    )
-    back = lax.all_to_all(slopes, "tile", split_axis=0, concat_axis=0, tiled=True)
+    )(got, state.reshape(species, planes, columns), edge_z, edge_y)
+    back = pl.pallas_call(
+        functools.partial(return_kernel, tiles),
+        out_shape=shape_of(tiles, 3, slot),
+        in_specs=[VMEM],
+        out_specs=VMEM,
+        scratch_shapes=[
+            pltpu.VMEM((tiles, 3, slot), jnp.float32),
+            pltpu.SemaphoreType.DMA((tiles,)),
+            pltpu.SemaphoreType.DMA((tiles,)),
+        ],
+        compiler_params=remote(2),
+    )(slopes)
     velocity = pl.pallas_call(
         functools.partial(unpack_kernel, tiles, slot),
         out_shape=shape_of(3, capacity),

time: 189 us -> 113 us (0.60)
  starting transfers between devices: 64.6 us -> 0 us
  Pallas kernels: 63.9 us -> 104 us
  waiting for transfers between devices: 20.3 us -> 0 us
  blocking collectives: 13.7 us -> 0 us
  other arithmetic: 12.1 us -> 2.9 us
  local copies, waits for them, and re-layouts: 11.5 us -> 4.31 us
    ppermute x22 -> x0, starting transfers between devices: 58.7 us -> none  [the longest x11 44.3 us: neighbours(): lax.ppermute(lax.slice_in_dim(block, block.shape[dim] - width, None, axis...]
    pallas_call x1 -> x3, Pallas kernels: 14.5 us -> 55.4 us  [the longest x1 37.4 us: local(): pl.pallas_call(functools.partial(diffuse_kernel, slabs, tiles), out_shape...]
    ppermute x22 -> x0, waiting for transfers between devices: 20.3 us -> none  [the longest x11 13.3 us: neighbours(): lax.ppermute(lax.slice_in_dim(block, block.shape[dim] - width, None, axis...]
    all_to_all x1 -> x0, blocking collectives: 13.7 us -> none  [local(): lax.all_to_all(packed, 'tile', split_axis=0, concat_axis=0, tiled=True)]
    sub x4 -> x0, other arithmetic: 9.36 us -> none  [relax(): return center + spread * (around - 6.0 * center) - losses * center]
    all_to_all x1 -> x0, starting transfers between devices: 5.9 us -> none  [local(): lax.all_to_all(slopes, 'tile', split_axis=0, concat_axis=0, tiled=True)]
    slice x11 -> x0, local copies, waits for them, and re-layouts: 3.5 us -> none  [the longest x10 2.89 us: neighbours(): lax.slice_in_dim(block, 0, width, axis=dim)]
    unnamed x22 -> x6, local copies, waits for them, and re-layouts: 6.6 us -> 4.31 us
  transfers between devices with their start and end apart: 23 -> 0, of which waited for: 8 -> 0; matrix products, arithmetic and copies ran while one was open for 3% -> 0% of each run, Pallas kernels for 18% -> 0%
where the time goes in v2:
time: 113 us
  Pallas kernels  104 us (92%)
  local copies, waits for them, and re-layouts  4.31 us (4%)
  other arithmetic  2.9 us (3%)
  between operations  1.35 us (1%)
    pallas_call x1, Pallas kernels, local(): pl.pallas_call(functools.partial(diffuse_kernel, slabs, tiles), out_shape...  37.4 us
    pallas_call x1, Pallas kernels, local(): pl.pallas_call(deposit_kernel, out_shape=shape_of(species, planes, column...  28.7 us
    pallas_call x1, Pallas kernels, local(): pl.pallas_call(functools.partial(slope_kernel, depth, rows), out_shape=sh...  18.3 us
    pallas_call x1, Pallas kernels, local(): pl.pallas_call(functools.partial(return_kernel, tiles), out_shape=shape_o...  9.41 us
    pallas_call x1, Pallas kernels, local(): pl.pallas_call(functools.partial(meet_kernel, tiles), out_shape=(shape_of...  8.59 us
    unnamed x6, local copies, waits for them, and re-layouts  4.31 us

profile of v2, /device:TPU:0, one launch (start us, length us, event | category | flops | bytes accessed | tf_op | source)
XLA Modules:
  0.0 112.9 jit_solution(17366099549943747050)
XLA Ops:
  1.3 0.7 fusion
  2.0 0.7 convert_element_type.5
  2.7 0.8 copy.10.chosen
  3.4 0.8 pad_maximum_fusion.table
  4.2 0.7 select_maximum_fusion.cells
  4.9 0.0 copy-start.1
  5.0 0.6 copy-done.1
  5.6 0.7 shard_map.95.packed
  6.3 8.6 %shard_map.96 = (f32[8,2,512]{2,1,0:T(2,128)S(1)}, f32[24,8,128]{2,1,0:T(8,128)S(1)}) custom-call(f32[8,2,512]{2,1,0:T(2,128)S(1)} %shard_map.95.packed, f32[4,2048]{1,0:T(4,128)S(1)} %pad_maximum_fusion.table), custom_call_target="tpu_custom_call" | custom-call | tf_op jit(solution)/shard_map/pallas_call | solution.py:456
  14.9 0.0 copy-start
  14.9 1.6 %copy-done = f32[2,8,16,2048]{3,2,1,0:T(8,128)S(1)} copy-done((f32[2,8,16,2048]{3,2,1,0:T(8,128)S(1)}, f32[2,8,16,2048]{3,2,1,0:T(8,128)}, u32[]{:S(2)}) %copy-start) | copy-done | bytes 2097176
  16.5 28.7 %shard_map.97 = f32[2,128,2048]{2,1,0:T(8,128)S(1)} custom-call(f32[8,2,512]{2,1,0:T(2,128)S(1)} %get-tuple-element.8.got, f32[2,128,2048]{2,1,0:T(8,128)S(1)} %bitcast.10), custom_call_target="tpu_custom_call" | custom-call | tf_op jit(solution)/shard_map/pallas_call | solution.py:471
  45.2 37.4 %shard_map.98 = (f32[2,8,16,2048]{3,2,1,0:T(8,128)S(1)}, f32[8,2048]{1,0:T(8,128)S(1)}, f32[2,16,2048]{2,1,0:T(8,128)S(1)}, f32[2,8,2048]{2,1,0:T(8,128)S(1)}) custom-call(s32[16,8]{1,0:T(8,128)S(1)} %copy.10.chosen, f32[24,8,128]{2,1,0:T(8,128)S(1)} %get-tuple-element.9.table, f32[2,8,16,2048]{3,2,1,0:T(8,128)S(1)} %bitcast.9), custom_call_target="tpu_custom_call" | custom-call | tf_op jit(solution)/shard_map/pallas_call | solution.py:480
  82.5 18.3 %shard_map.99.slopes = f32[8,3,512]{2,1,0:T(4,128)S(1)} custom-call(f32[8,2,512]{2,1,0:T(2,128)S(1)} %get-tuple-element.8.got, f32[2,128,2048]{2,1,0:T(8,128)S(1)} %bitcast.8, f32[2,16,2048]{2,1,0:T(8,128)S(1)} %get-tuple-element.11.edge_z, f32[2,8,2048]{2,1,0:T(8,128)S(1)} %get-tuple-element.12.edge_y), custom_call_target="tpu_custom_call" | custom-call | tf_op jit(solution)/shard_map/pallas_call | solution.py:502
  100.9 9.4 %shard_map.100.back = f32[8,3,512]{2,1,0:T(4,128)S(1)} custom-call(f32[8,3,512]{2,1,0:T(4,128)S(1)} %shard_map.99.slopes), custom_call_target="tpu_custom_call" | custom-call | tf_op jit(solution)/shard_map/pallas_call | solution.py:512
  110.3 1.3 %shard_map.101 = f32[3,2048]{1,0:T(4,128)} custom-call(s32[1,8]{1,0:T(1,128)S(1)} %copy-done.1, f32[8,3,512]{2,1,0:T(4,128)S(1)} %shard_map.100.back, f32[8,2048]{1,0:T(8,128)S(1)} %get-tuple-element.13.force), custom_call_target="tpu_custom_call" | custom-call | tf_op jit(solution)/shard_map/pallas_call | solution.py:524
  111.6 1.3 %copy.13 = f32[2,8,16,2048]{3,2,1,0:T(8,128)} copy(f32[2,8,16,2048]{3,2,1,0:T(8,128)S(1)} %get-tuple-element.17) | data formatting | bytes 4194304
Async XLA Ops:
  4.9 0.7 copy-start.1
  14.9 1.6 %copy-start = (f32[2,8,16,2048]{3,2,1,0:T(8,128)S(1)}, f32[2,8,16,2048]{3,2,1,0:T(8,128)}, u32[]{:S(2)}) copy-start(f32[2,8,16,2048]{3,2,1,0:T(8,128)} %param.15) | copy-start | bytes 6291460

commit v3 on v2

--- a/solution.py
+++ b/solution.py
@@ -287,8 +287,6 @@
         return made
 
     def begin(step, now, which):
-        for up in range(2):
-            sent_y[step, up] = state[now, :, 1 : depth + 1, (rows - 1) * up, :]
         made = copies(step, now, which)
         for n in (2, 3, 0, 1):
 
@@ -296,12 +294,11 @@
             def _(n=n):
                 made[n].start()
 
-        return made
-
-    def finish(made):
-        for n, side in enumerate(sides):
-
-            @pl.when(exists(side))
+    def finish(step, now, which, axis):
+        made = copies(step, now, which)
+        for n in (2 * axis, 2 * axis + 1):
+
+            @pl.when(exists(sides[n]))
             def _(n=n):
                 made[n].wait_send()
                 made[n ^ 1].wait_recv()
@@ -316,15 +313,19 @@
     lane = lax.broadcasted_iota(jnp.int32, (rows, columns), 1)
     row = lax.broadcasted_iota(jnp.int32, (rows, columns), 0)
 
-    def one_step(step, carry):
+    both = slice(0, species)
+    for up in range(2):
+        sent_y[0, up] = state[0, :, 1 : depth + 1, (rows - 1) * up, :]
+    begin(0, 0, both)
+    widen(table, wide)
+
+    def settle(later, step, s, up, z):
+        edge = slice((rows - 1) * up, (rows - 1) * up + 1)
+        state[later, s, z, edge] = sent_y[step + 1, up, s, z - 1 : z]
+
+    def one_step(step, after):
         now = lax.rem(step, 2)
         later = 1 - now
-        made = begin(step, now, slice(0, species))
-
-        @pl.when(step == 0)
-        def _():
-            widen(table, wide)
-
         for s in range(species):
 
             def one_plane(z, carry):
@@ -339,26 +340,45 @@
 
             lax.fori_loop(1, depth + 1, one_plane, 0)
         force_blocks(chosen, table, wide, force, step * share, (step + 1) * share)
-        finish(made)
+        for up in range(2):
+            sent_y[step + 1, up] = state[later, :, 1 : depth + 1, (rows - 1) * up, :]
+        finish(step, now, both, 0)
+        for s in range(species):
+            for side, z in enumerate((1, depth)):
+                state[later, s, z] += DIFFUSION[s] * halo_z[step, side, s]
+                for up in range(2):
+                    edge = slice((rows - 1) * up, (rows - 1) * up + 1)
+                    sent_y[step + 1, up, s, z - 1 : z] += (
+                        DIFFUSION[s] * halo_z[step, side, s, edge]
+                    )
+        finish(step, now, both, 1)
         for s in range(species):
             for up in range(2):
-                state[later, s, depth if up else 1] += DIFFUSION[s] * halo_z[step, up, s]
-                for z in range(depth):
-                    edge = slice((rows - 1) * up, (rows - 1) * up + 1)
-                    state[later, s, z + 1, edge] += DIFFUSION[s] * halo_y[step, up, s, z : z + 1]
+                sent_y[step + 1, up, s] += DIFFUSION[s] * halo_y[step, up, s]
+                for z in (1, depth):
+                    settle(later, step, s, up, z)
+        begin(step + 1, later, after)
+        for s in range(species):
+            for up in range(2):
+                for z in range(2, depth):
+                    settle(later, step, s, up, z)
+
+    def earlier(step, carry):
+        one_step(step, both)
         return carry
 
-    lax.fori_loop(0, ITERS, one_step, 0)
+    lax.fori_loop(0, ITERS - 1, earlier, 0)
+    one_step(jnp.int32(ITERS - 1), 1)
     last = ITERS % 2
-    made = begin(ITERS, last, 1)
     force_blocks(chosen, table, wide, force, ITERS * share, blocks)
     out[...] = state[last, :, 1 : depth + 1]
-    finish(made)
+    finish(ITERS, last, 1, 0)
+    finish(ITERS, last, 1, 1)
     edge_z[...] = halo_z[ITERS, :, 1]
     edge_y[...] = halo_y[ITERS, :, 1]
 
 
-def deposit_kernel(got, field, out, oxygen):
+def deposit_kernel(got, field, out, oxygen, weights):
     tiles = got.shape[0]
     planes, columns = field.shape[1:]
     out[...] = field[...]
@@ -370,7 +390,9 @@
         wanted = got[t, 0:1].astype(jnp.int32)
         given = got[t, 1:2]
         row_hot = hot(wanted // columns, planes)
-        column_hot = hot(wanted % columns, columns).astype(jnp.bfloat16)
+        lines = lax.broadcasted_iota(jnp.int32, (columns, wanted.shape[1]), 0).astype(jnp.int16)
+        here = lines == (wanted % columns).astype(jnp.int16)
+        column_hot = jnp.where(here, jnp.bfloat16(1), jnp.bfloat16(0))
         picked = dot(oxygen[...], column_hot, (1, 0))
         picked = picked[:planes] + picked[planes:]
         o = jnp.sum(jnp.where(row_hot, picked, 0.0), axis=0, keepdims=True)
@@ -378,30 +400,44 @@
         secrete = SECRETION * given * HYPOXIA_HALF / (HYPOXIA_HALF + o)
         for s, amount in enumerate((-STEP_TIME * consume, STEP_TIME * secrete)):
             high, low = halves(jnp.where(row_hot, amount, 0.0))
-            out[s] += dot(high, column_hot, (1, 1)) + dot(low, column_hot, (1, 1))
+            weights[s * planes : (s + 1) * planes] = high
+            weights[(s + 2) * planes : (s + 3) * planes] = low
+        added = dot(weights[...], column_hot, (1, 1))
+        for s in range(2):
+            out[s] += (
+                added[s * planes : (s + 1) * planes] + added[(s + 2) * planes : (s + 3) * planes]
+            )
         return carry
 
-    lax.fori_loop(0, tiles, one_source, 0)
+    lax.fori_loop(0, tiles, one_source, 0, unroll=2)
 
 
 def slope_kernel(depth, rows, got, field, edge_z, edge_y, out, near):
     tiles = got.shape[0]
     planes, columns = field.shape[1:]
     count = planes + 2 * rows + 2 * depth
+    total = count + planes
+    vegf = field[1]
+    lane = lax.broadcasted_iota(jnp.int32, vegf.shape, 1)
+    right = jnp.where(lane == columns - 1, 0.0, pltpu.roll(vegf, columns - 1, 1))
+    left = jnp.where(lane == 0, 0.0, pltpu.roll(vegf, 1, 1))
     first = 0
-    for part in (edge_z[0], field[1], edge_z[1], edge_y[0], edge_y[1]):
+    edges = jnp.concatenate([edge_y[0], edge_y[1]], axis=0)
+    for part in (edge_z[0], vegf, edge_z[1], edges, right - left):
         high, low = halves(part)
         near[first : first + part.shape[0]] = high
-        near[count + first : count + first + part.shape[0]] = low
+        near[total + first : total + first + part.shape[0]] = low
         first += part.shape[0]
 
     def one_source(t, carry):
         wanted = got[t, 0:1].astype(jnp.int32)
-        row, column = wanted // columns, wanted % columns
+        row = wanted // columns
         z, y = row // rows, row % rows
-        inner = hot(column, columns).astype(jnp.bfloat16)
-        values = dot(near[...], inner, (1, 0))
-        values = values[:count] + values[count:]
+        column_hot = hot(wanted % columns, columns).astype(jnp.bfloat16)
+        values = dot(near[...], column_hot, (1, 0))
+        values = values[:total] + values[total:]
+        change = jnp.where(hot(row, planes), values[count:], 0.0)
+        values = values[:count]
 
         def at(index):
             return jnp.sum(jnp.where(hot(index, count), values, 0.0), axis=0, keepdims=True)
@@ -410,15 +446,10 @@
         above = jnp.where(y == rows - 1, planes + 2 * rows + depth + z, row + rows + 1)
         out[t, 0:1] = 0.5 * (at(row + 2 * rows) - at(row))
         out[t, 1:2] = 0.5 * (at(above) - at(below))
-        right = jnp.where(hot(column + 1, columns), 1.0, 0.0)
-        beside = jnp.where(hot(column - 1, columns), -1.0, right).astype(jnp.bfloat16)
-        change = dot(near[rows : rows + planes], beside, (1, 0))
-        change = change + dot(near[count + rows : count + rows + planes], beside, (1, 0))
-        change = jnp.where(hot(row, planes), change, 0.0)
         out[t, 2:3] = 0.5 * jnp.sum(change, axis=0, keepdims=True)
         return carry
 
-    lax.fori_loop(0, tiles, one_source, 0)
+    lax.fori_loop(0, tiles, one_source, 0, unroll=2)
 
 
 def remote(number):
@@ -473,7 +504,10 @@
         out_shape=shape_of(species, planes, columns),
         in_specs=[VMEM, VMEM],
         out_specs=VMEM,
-        scratch_shapes=[pltpu.VMEM((2 * planes, columns), jnp.bfloat16)],
+        scratch_shapes=[
+            pltpu.VMEM((2 * planes, columns), jnp.bfloat16),
+            pltpu.VMEM((4 * planes, slot), jnp.bfloat16),
+        ],
         compiler_params=LIMIT,
     )(got, field.reshape(species, planes, columns))
     steps = ITERS + 1
@@ -505,7 +539,7 @@
         in_specs=[VMEM] * 4,
         out_specs=VMEM,
         scratch_shapes=[
-            pltpu.VMEM((2 * (planes + 2 * rows + 2 * depth), columns), jnp.bfloat16)
+            pltpu.VMEM((4 * (planes + rows + depth), columns), jnp.bfloat16)
         ],
         compiler_params=LIMIT,
     )(got, state.reshape(species, planes, columns), edge_z, edge_y)

time: 113 us -> 94.5 us (0.84)
  Pallas kernels: 104 us -> 85.5 us
    pallas_call x1, Pallas kernels: 28.7 us -> 15.4 us  [local(): pl.pallas_call(deposit_kernel, out_shape=shape_of(species, planes, column...]
    pallas_call x1, Pallas kernels: 18.3 us -> 13.4 us  [local(): pl.pallas_call(functools.partial(slope_kernel, depth, rows), out_shape=sh...]
where the time goes in v3:
time: 94.5 us; the launch traced here: 94.1 us
  Pallas kernels  85.5 us (90%)
  local copies, waits for them, and re-layouts  4.31 us (5%)
  other arithmetic  2.9 us (3%)
  between operations  1.35 us (1%)
    pallas_call x1, Pallas kernels, local(): pl.pallas_call(functools.partial(diffuse_kernel, slabs, tiles), out_shape...  36.7 us
    pallas_call x1, Pallas kernels, local(): pl.pallas_call(deposit_kernel, out_shape=shape_of(species, planes, column...  15.4 us
    pallas_call x1, Pallas kernels, local(): pl.pallas_call(functools.partial(slope_kernel, depth, rows), out_shape=sh...  13.4 us
    pallas_call x1, Pallas kernels, local(): pl.pallas_call(functools.partial(return_kernel, tiles), out_shape=shape_o...  9.4 us
    pallas_call x1, Pallas kernels, local(): pl.pallas_call(functools.partial(meet_kernel, tiles), out_shape=(shape_of...  8.59 us
    unnamed x6, local copies, waits for them, and re-layouts  4.31 us

profile of v3, /device:TPU:0, one launch (start us, length us, event | category | flops | bytes accessed | tf_op | source)
XLA Modules:
  0.0 94.1 jit_solution(9102703657782186145)
XLA Ops:
  1.3 0.7 fusion
  2.0 0.7 convert_element_type.5
  2.7 0.8 copy.10.chosen
  3.4 0.8 pad_maximum_fusion.table
  4.2 0.7 select_maximum_fusion.cells
  4.9 0.0 copy-start.1
  5.0 0.6 copy-done.1
  5.6 0.7 shard_map.95.packed
  6.3 8.6 %shard_map.96 = (f32[8,2,512]{2,1,0:T(2,128)S(1)}, f32[24,8,128]{2,1,0:T(8,128)S(1)}) custom-call(f32[8,2,512]{2,1,0:T(2,128)S(1)} %shard_map.95.packed, f32[4,2048]{1,0:T(4,128)S(1)} %pad_maximum_fusion.table), custom_call_target="tpu_custom_call" | custom-call | tf_op jit(solution)/shard_map/pallas_call | solution.py:487
  14.9 0.0 copy-start
  14.9 1.6 %copy-done = f32[2,8,16,2048]{3,2,1,0:T(8,128)S(1)} copy-done((f32[2,8,16,2048]{3,2,1,0:T(8,128)S(1)}, f32[2,8,16,2048]{3,2,1,0:T(8,128)}, u32[]{:S(2)}) %copy-start) | copy-done | bytes 2097176
  16.5 15.4 %shard_map.97 = f32[2,128,2048]{2,1,0:T(8,128)S(1)} custom-call(f32[8,2,512]{2,1,0:T(2,128)S(1)} %get-tuple-element.8.got, f32[2,128,2048]{2,1,0:T(8,128)S(1)} %bitcast.10), custom_call_target="tpu_custom_call" | custom-call | tf_op jit(solution)/shard_map/pallas_call | solution.py:502
  31.9 36.7 %shard_map.98 = (f32[2,8,16,2048]{3,2,1,0:T(8,128)S(1)}, f32[8,2048]{1,0:T(8,128)S(1)}, f32[2,16,2048]{2,1,0:T(8,128)S(1)}, f32[2,8,2048]{2,1,0:T(8,128)S(1)}) custom-call(s32[16,8]{1,0:T(8,128)S(1)} %copy.10.chosen, f32[24,8,128]{2,1,0:T(8,128)S(1)} %get-tuple-element.9.table, f32[2,8,16,2048]{3,2,1,0:T(8,128)S(1)} %bitcast.9), custom_call_target="tpu_custom_call" | custom-call | tf_op jit(solution)/shard_map/pallas_call | solution.py:514
  68.6 13.4 %shard_map.99.slopes = f32[8,3,512]{2,1,0:T(4,128)S(1)} custom-call(f32[8,2,512]{2,1,0:T(2,128)S(1)} %get-tuple-element.8.got, f32[2,128,2048]{2,1,0:T(8,128)S(1)} %bitcast.8, f32[2,16,2048]{2,1,0:T(8,128)S(1)} %get-tuple-element.11.edge_z, f32[2,8,2048]{2,1,0:T(8,128)S(1)} %get-tuple-element.12.edge_y), custom_call_target="tpu_custom_call" | custom-call | tf_op jit(solution)/shard_map/pallas_call | solution.py:536
  82.0 9.4 %shard_map.100.back = f32[8,3,512]{2,1,0:T(4,128)S(1)} custom-call(f32[8,3,512]{2,1,0:T(4,128)S(1)} %shard_map.99.slopes), custom_call_target="tpu_custom_call" | custom-call | tf_op jit(solution)/shard_map/pallas_call | solution.py:546
  91.4 1.3 %shard_map.101 = f32[3,2048]{1,0:T(4,128)} custom-call(s32[1,8]{1,0:T(1,128)S(1)} %copy-done.1, f32[8,3,512]{2,1,0:T(4,128)S(1)} %shard_map.100.back, f32[8,2048]{1,0:T(8,128)S(1)} %get-tuple-element.13.force), custom_call_target="tpu_custom_call" | custom-call | tf_op jit(solution)/shard_map/pallas_call | solution.py:558
  92.8 1.3 %copy.13 = f32[2,8,16,2048]{3,2,1,0:T(8,128)} copy(f32[2,8,16,2048]{3,2,1,0:T(8,128)S(1)} %get-tuple-element.17) | data formatting | bytes 4194304
Async XLA Ops:
  4.9 0.7 copy-start.1
  14.9 1.6 %copy-start = (f32[2,8,16,2048]{3,2,1,0:T(8,128)S(1)}, f32[2,8,16,2048]{3,2,1,0:T(8,128)}, u32[]{:S(2)}) copy-start(f32[2,8,16,2048]{3,2,1,0:T(8,128)} %param.15) | copy-start | bytes 6291460
